TPU v7x, 256 devices: a whole 4x4x8 slice. The times are simulated.
256 devices in a mesh: tm: 16 (over y, z_lo, core), space: 16 (over x, z_hi).
Axes of the slice: x: 4, y: 4, z: 8 (z_hi: 4, z_lo: 2; z = z_hi * 2 + z_lo), core: 2. Of those that a mesh axis runs over, the one named last changes fastest.
Arguments:
- checkpoints: float32 [16, 64, 128, 128], P('tm', 'space'), may hold values from -1 to 1
- guess: float32 [16, 64, 128, 128], P('tm', 'space'), may hold values from -6 to 6
- materials: int32 [64, 128, 128], P('space'), may hold values from 0 to 7
- table: float32 [8], replicated, may hold values from 0.5 to 2
- weight: float32 [64, 128, 128], P('space'), may hold values from 0.2 to 2
Outputs:
- corrected: float32 [16, 64, 128, 128], P('tm', 'space')
- sensitivity: float32 [64, 128, 128], P('space', None, 'tm')
All inputs are finite; a program needn't handle non-finite values.
Results may differ from a plain program's by a relative error of at most 0.00002.
Values sent between devices are 32-bit elements; how exact they have to be, the bound alone decides.
A program may use at most 128 MiB of HBM per device.

v0:
```python
import jax
import jax.numpy as jnp
from jax import lax
from jax.sharding import PartitionSpec as P

COARSEN = 8


fine_rate = 0.006
conduct_slope = 0.5


def with_halo(shard, sides, width):
    for axis, dim in sides:
        peers, length = (lax.axis_size(axis), shard.shape[dim])
        up = [(i, (i + 1) % peers) for i in range(peers - 1)]
        down = [(j, i) for i, j in up]
        last = lax.slice_in_dim(shard, length - width, length, axis=dim)
        first = lax.slice_in_dim(shard, 0, width, axis=dim)
        before = lax.ppermute(last, axis, up)
        after = lax.ppermute(first, axis, down)
        shard = jnp.concatenate([before, shard, after], axis=dim)
    return shard


def shifted(block, axis, distance):
    devices = range(lax.axis_size(axis))
    route = [(i - distance, i) for i in devices if i - distance in devices]
    return lax.ppermute(block, axis, route)


def widen(field):
    return jnp.pad(field, [(0, 0)] * (field.ndim - 2) + [(1, 1), (1, 1)])


def neighbours(padded):
    centre = padded[..., 1:-1, 1:-1, 1:-1]
    beside_all = [
        padded[..., 2:, 1:-1, 1:-1],
        padded[..., :-2, 1:-1, 1:-1],
        padded[..., 1:-1, 2:, 1:-1],
        padded[..., 1:-1, :-2, 1:-1],
        padded[..., 1:-1, 1:-1, 2:],
        padded[..., 1:-1, 1:-1, :-2],
    ]
    return (centre, beside_all)


def conductivity(materials, table):
    result = jnp.zeros(materials.shape, jnp.float32)
    for number in range(table.shape[0]):
        result = result + jnp.where(materials == number, table[number], 0.0)
    return result


def forward_step(temp_ext, base_ext):
    heat, heat_side = neighbours(widen(temp_ext))
    conduct, conduct_side = neighbours(widen(base_ext * (1.0 + conduct_slope * temp_ext)))
    flow = jnp.zeros_like(heat)
    for other_heat, other_cond in zip(heat_side, conduct_side):
        flow = flow + 0.5 * (conduct + other_cond) * (other_heat - heat)
    return heat + fine_rate * flow


def adjoint_step(adjoint_ext, temp_ext, base_ext, factor):
    latest, latest_side = neighbours(widen(adjoint_ext))
    heat, heat_side = neighbours(widen(temp_ext))
    conduct, conduct_side = neighbours(widen(base_ext * (1.0 + conduct_slope * temp_ext)))
    base_mid = base_ext[..., 1:-1, :, :]
    flow = jnp.zeros_like(latest)
    spread = jnp.zeros_like(latest)
    for other_adj, other_heat, other_cond in zip(latest_side, heat_side, conduct_side):
        flow = flow + 0.5 * (conduct + other_cond) * (other_adj - latest)
        spread = spread + (other_heat - heat) * (latest - other_adj)
    return (latest + factor * flow + 0.5 * factor * conduct_slope * base_mid * spread, spread)


def on_device(checkpoints, guess, materials, table, weight):
    intervals = guess.shape[0]
    coarse_rate = COARSEN * fine_rate
    base = conductivity(materials, table)
    base_ext = with_halo(base, (("space", 0),), 1)
    temps = []
    current = checkpoints
    for offset in range(COARSEN):
        padded = with_halo(current, (("space", 1),), 1)
        temps.append(padded)
        if offset + 1 < COARSEN:
            current = forward_step(padded, base_ext)
    upper = shifted(guess, "tm", -1)
    latest = jnp.concatenate([guess[1:], upper], 0)
    for offset in reversed(range(COARSEN)):
        padded = with_halo(latest, (("space", 1),), 1)
        stepped = adjoint_step(padded, temps[offset], base_ext, fine_rate)[0]
        latest = stepped + weight * temps[offset][:, 1:-1]
    residual = latest - guess
    coarse_temp = temps[0]

    def section(rounds, holding):
        leading, _ = holding
        incoming = shifted(leading, "tm", -1)
        pieces = [None] * intervals
        error = incoming
        for local in reversed(range(intervals)):
            padded = with_halo(error, (("space", 0),), 1)
            error = (
                adjoint_step(padded, coarse_temp[local], base_ext, coarse_rate)[0] + residual[local]
            )
            pieces[local] = error
        return (error, jnp.stack(pieces, 0))

    _, errors = lax.fori_loop(
        0, lax.axis_size("tm"), section, (jnp.zeros_like(guess[0]), jnp.zeros_like(guess))
    )
    corrected = guess + errors
    upper_corr = shifted(corrected, "tm", -1)
    latest = jnp.concatenate([corrected[1:], upper_corr], 0)
    total = jnp.zeros_like(guess[0])
    for offset in reversed(range(COARSEN)):
        padded = with_halo(latest, (("space", 1),), 1)
        stepped, spread = adjoint_step(padded, temps[offset], base_ext, fine_rate)
        heat = temps[offset][:, 1:-1]
        total = total + jnp.sum(0.5 * fine_rate * (1.0 + conduct_slope * heat) * spread, 0)
        latest = stepped + weight * heat
    sensitivity = lax.psum_scatter(total, "tm", scatter_dimension=2, tiled=True)
    return (corrected, sensitivity)


def solution(mesh):
    in_specs = (
        P("tm", "space", None, None),
        P("tm", "space", None, None),
        P("space", None, None),
        P(),
        P("space", None, None),
    )
    out_specs = (P("tm", "space", None, None), P("space", None, "tm"))
    return jax.shard_map(
        on_device, mesh=mesh, in_specs=in_specs, out_specs=out_specs, check_vma=False
    )
```

profile of v0, /device:TPU:17, one launch (start us, length us, event | category | flops | bytes accessed | tf_op | source)
XLA Modules:
  0.0 911.8 jit_solution(789431336779921017)
XLA Ops:
  21.7 6.7 collective-permute-start.3
  44.3 6.5 collective-permute-done.9
  95.0 9.2 %collective-permute-start.7 = (f32[1,4,128,128]{2,3,1,0:T(8,128)}, f32[1,4,128,128]{2,3,1,0:T(8,128)}, u32[]{:S(2)}, u32[]{:S(2)}) collective-permute-start(f32[1,4,128,128]{2,3,1,0:T(8,128)} %copy.22), channel_id=1, source_target_pairs={{16,0},{32,16},{48,32},{64,48},{80,64},{96,80},{112,96},{128,112},... | collective-permute-start | bytes 786440 | tf_op jit(solution)/shard_map/ppermute | solution.py:29
  117.1 6.8 collective-permute-start.23
  136.5 7.1 fusion.491
  160.0 6.7 collective-permute-start.27
  168.3 6.8 fusion.443
  176.5 7.4 collective-permute-start.29
  192.7 6.7 collective-permute-start.31
  208.4 6.6 collective-permute-start.33
  225.2 7.1 collective-permute-start.35
  239.3 6.9 fusion.351
  248.9 6.4 collective-permute-start.37
  259.5 7.7 fusion.328
  269.0 427.3 %while.15 = (s32[]{:T(128)}, f32[4,128,128]{2,1,0:T(8,128)S(1)}, f32[1,4,128,128]{3,2,1,0:T(8,128)}, f32[1,6,128,128]{3,2,1,0:T(8,128)S(1)}, f32[6,128,128]{2,1,...) while((s32[]{:T(128)}, f32[4,128,128]{2,1,0:T(8,128)S(1)}, ...), condition=%wide.region_1.2_spmd.clone, body=%wide.region_0.1_spmd.clone.sunk | while | flops 5682539 | bytes 16265719 | solution.py:112
  269.0 10.1 %collective-permute-start = (f32[4,128,128]{2,1,0:T(8,128)S(1)}, f32[4,128,128]{2,1,0:T(8,128)S(1)}, u32[]{:S(2)}, u32[]{:S(2)}) collective-permute-start(f32[4,128,128]{2,1,0:T(8,128)S(1)} %broadcast_select_fusion.2), channel_id=1, source_target_pairs={{16,0},{32,16},{48,32},{64,48},{80,64},{96,80},{112,96},{128,112},... | collective-permute-start | bytes 786440 | tf_op jit(solution)/shard_map/while/body/eval_jaxpr/ppermute | solution.py:29
  283.6 7.0 collective-permute-start.1
  292.0 8.4 collective-permute-done.2
  314.2 7.3 collective-permute-start.1
  323.1 8.4 collective-permute-done.2
  345.2 6.3 collective-permute-start.1
  352.9 6.5 collective-permute-done.2
  464.6 6.2 collective-permute-start
  648.3 6.4 collective-permute-done
  700.1 7.3 collective-permute-done.38
  737.5 6.6 collective-permute-start.44
  746.1 6.8 fusion.262
  754.3 6.3 collective-permute-start.46
  769.5 7.1 collective-permute-start.48
  785.6 6.6 collective-permute-start.50
  816.7 6.6 collective-permute-start.54
  826.4 78.6 %reduce-scatter.2.cloned.1.call-done = f32[4,128,8]{1,2,0:T(8,128)} async-done(((f32[4,128,128]{1,2,0:T(8,128)}), f32[4,128,8]{1,2,0:T(8,128)}) %reduce-scatter.2.cloned.1.call-update) | async-done | bytes 16400 | tf_op jit(solution)/shard_map/reduce_scatter | solution.py:125
  (752 shorter events, 602.8 us)
Async XLA Ops:
  7.2 897.8 %reduce-scatter.2.cloned.1.call-start = ((), (), s32[]{:S(2)}) async-start(), calls=%async_computation.1 | async-start | bytes 278528 | tf_op jit(solution)/shard_map/reduce_scatter | solution.py:125
  15.2 19.8 %collective-permute-start.5 = (f32[1,128,128]{1,2,0:T(8,128)S(1)}, f32[1,128,128]{1,2,0:T(8,128)S(1)}, u32[]{:S(2)}, u32[]{:S(2)}) collective-permute-start(f32[1,128,128]{1,2,0:T(8,128)S(1)} %get-tuple-element.236), channel_id=1, source_target_pairs={{0,1},{1,2},{2,3},{3,4},{4,5},{5,6},{6,7},{7,8},{8,9},{9,10},{10,1... | collective-permute-start | bytes 196616 | tf_op jit(solution)/shard_map/ppermute | solution.py:20
  20.2 14.8 %collective-permute-start.6 = (f32[1,128,128]{1,2,0:T(8,128)S(1)}, f32[1,128,128]{1,2,0:T(8,128)S(1)}, u32[]{:S(2)}, u32[]{:S(2)}) collective-permute-start(f32[1,128,128]{1,2,0:T(8,128)S(1)} %get-tuple-element.237), channel_id=1, source_target_pairs={{1,0},{2,1},{3,2},{4,3},{5,4},{6,5},{7,6},{8,7},{9,8},{10,9},{11,1... | collective-permute-start | bytes 196616 | tf_op jit(solution)/shard_map/ppermute | solution.py:21
  21.7 13.3 %collective-permute-start.3 = (f32[1,1,128,128]{2,3,1,0:T(8,128)S(1)}, f32[1,1,128,128]{2,3,1,0:T(8,128)S(1)}, u32[]{:S(2)}, u32[]{:S(2)}) collective-permute-start(f32[1,1,128,128]{2,3,1,0:T(8,128)S(1)} %get-tuple-element.238), channel_id=1, source_target_pairs={{0,1},{1,2},{2,3},{3,4},{4,5},{5,6},{6,7},{7,8},{8,9},{9,10},{10,1... | collective-permute-start | bytes 196616 | tf_op jit(solution)/shard_map/ppermute | solution.py:20
  88.5 16.8 %collective-permute-start.16 = (f32[1,1,128,128]{2,3,1,0:T(8,128)}, f32[1,1,128,128]{2,3,1,0:T(8,128)S(1)}, u32[]{:S(2)}, u32[]{:S(2)}) collective-permute-start(f32[1,1,128,128]{2,3,1,0:T(8,128)} %get-tuple-element.224), channel_id=1, source_target_pairs={{0,1},{1,2},{2,3},{3,4},{4,5},{5,6},{6,7},{7,8},{8,9},{9,10},{10,1... | collective-permute-start | bytes 196616 | tf_op jit(solution)/shard_map/ppermute | solution.py:20
  92.8 13.1 %collective-permute-start.17 = (f32[1,1,128,128]{2,3,1,0:T(8,128)S(1)}, f32[1,1,128,128]{2,3,1,0:T(8,128)}, u32[]{:S(2)}, u32[]{:S(2)}) collective-permute-start(f32[1,1,128,128]{2,3,1,0:T(8,128)S(1)} %get-tuple-element.225), channel_id=1, source_target_pairs={{1,0},{2,1},{3,2},{4,3},{5,4},{6,5},{7,6},{8,7},{9,8},{10,9},{11,1... | collective-permute-start | bytes 196616 | tf_op jit(solution)/shard_map/ppermute | solution.py:21
  95.0 19.9 %collective-permute-start.7 = (f32[1,4,128,128]{2,3,1,0:T(8,128)}, f32[1,4,128,128]{2,3,1,0:T(8,128)}, u32[]{:S(2)}, u32[]{:S(2)}) collective-permute-start(f32[1,4,128,128]{2,3,1,0:T(8,128)} %copy.22), channel_id=1, source_target_pairs={{16,0},{32,16},{48,32},{64,48},{80,64},{96,80},{112,96},{128,112},... | collective-permute-start | bytes 786440 | tf_op jit(solution)/shard_map/ppermute | solution.py:29
  108.4 15.5 %collective-permute-start.18 = (f32[1,1,128,128]{2,3,1,0:T(8,128)S(1)}, f32[1,1,128,128]{2,3,1,0:T(8,128)S(1)}, u32[]{:S(2)}, u32[]{:S(2)}) collective-permute-start(f32[1,1,128,128]{2,3,1,0:T(8,128)S(1)} %get-tuple-element.222), channel_id=1, source_target_pairs={{0,1},{1,2},{2,3},{3,4},{4,5},{5,6},{6,7},{7,8},{8,9},{9,10},{10,1... | collective-permute-start | bytes 196616 | tf_op jit(solution)/shard_map/ppermute | solution.py:20
  113.6 10.4 %collective-permute-start.19 = (f32[1,1,128,128]{2,3,1,0:T(8,128)S(1)}, f32[1,1,128,128]{2,3,1,0:T(8,128)S(1)}, u32[]{:S(2)}, u32[]{:S(2)}) collective-permute-start(f32[1,1,128,128]{2,3,1,0:T(8,128)S(1)} %get-tuple-element.223), channel_id=1, source_target_pairs={{1,0},{2,1},{3,2},{4,3},{5,4},{6,5},{7,6},{8,7},{9,8},{10,9},{11,1... | collective-permute-start | bytes 196616 | tf_op jit(solution)/shard_map/ppermute | solution.py:21
  115.8 15.5 %collective-permute-start.22 = (f32[1,1,128,128]{2,3,1,0:T(8,128)S(1)}, f32[1,1,128,128]{2,3,1,0:T(8,128)S(1)}, u32[]{:S(2)}, u32[]{:S(2)}) collective-permute-start(f32[1,1,128,128]{2,3,1,0:T(8,128)S(1)} %get-tuple-element.234), channel_id=1, source_target_pairs={{1,0},{2,1},{3,2},{4,3},{5,4},{6,5},{7,6},{8,7},{9,8},{10,9},{11,1... | collective-permute-start | bytes 196616 | tf_op jit(solution)/shard_map/ppermute | solution.py:21
  117.1 14.2 %collective-permute-start.23 = (f32[1,1,128,128]{2,3,1,0:T(8,128)S(1)}, f32[1,1,128,128]{2,3,1,0:T(8,128)S(1)}, u32[]{:S(2)}, u32[]{:S(2)}) collective-permute-start(f32[1,1,128,128]{2,3,1,0:T(8,128)S(1)} %get-tuple-element.235), channel_id=1, source_target_pairs={{0,1},{1,2},{2,3},{3,4},{4,5},{5,6},{6,7},{7,8},{8,9},{9,10},{10,1... | collective-permute-start | bytes 196616 | tf_op jit(solution)/shard_map/ppermute | solution.py:20
  175.1 8.8 collective-permute-start.28
  176.5 8.6 collective-permute-start.29
  223.9 13.9 %collective-permute-start.34 = (f32[1,1,128,128]{2,3,1,0:T(8,128)}, f32[1,1,128,128]{2,3,1,0:T(8,128)}, u32[]{:S(2)}, u32[]{:S(2)}) collective-permute-start(f32[1,1,128,128]{2,3,1,0:T(8,128)} %get-tuple-element.208), channel_id=1, source_target_pairs={{1,0},{2,1},{3,2},{4,3},{5,4},{6,5},{7,6},{8,7},{9,8},{10,9},{11,1... | collective-permute-start | bytes 196616 | tf_op jit(solution)/shard_map/ppermute | solution.py:21
  225.2 12.7 %collective-permute-start.35 = (f32[1,1,128,128]{2,3,1,0:T(8,128)}, f32[1,1,128,128]{2,3,1,0:T(8,128)}, u32[]{:S(2)}, u32[]{:S(2)}) collective-permute-start(f32[1,1,128,128]{2,3,1,0:T(8,128)} %get-tuple-element.209), channel_id=1, source_target_pairs={{0,1},{1,2},{2,3},{3,4},{4,5},{5,6},{6,7},{7,8},{8,9},{9,10},{10,1... | collective-permute-start | bytes 196616 | tf_op jit(solution)/shard_map/ppermute | solution.py:20
  247.6 10.5 %collective-permute-start.36 = (f32[1,1,128,128]{2,3,1,0:T(8,128)}, f32[1,1,128,128]{2,3,1,0:T(8,128)}, u32[]{:S(2)}, u32[]{:S(2)}) collective-permute-start(f32[1,1,128,128]{2,3,1,0:T(8,128)} %get-tuple-element.206), channel_id=1, source_target_pairs={{1,0},{2,1},{3,2},{4,3},{5,4},{6,5},{7,6},{8,7},{9,8},{10,9},{11,1... | collective-permute-start | bytes 196616 | tf_op jit(solution)/shard_map/ppermute | solution.py:21
  248.9 9.2 %collective-permute-start.37 = (f32[1,1,128,128]{2,3,1,0:T(8,128)}, f32[1,1,128,128]{2,3,1,0:T(8,128)}, u32[]{:S(2)}, u32[]{:S(2)}) collective-permute-start(f32[1,1,128,128]{2,3,1,0:T(8,128)} %get-tuple-element.207), channel_id=1, source_target_pairs={{0,1},{1,2},{2,3},{3,4},{4,5},{5,6},{6,7},{7,8},{8,9},{9,10},{10,1... | collective-permute-start | bytes 196616 | tf_op jit(solution)/shard_map/ppermute | solution.py:20
  269.0 13.9 %collective-permute-start = (f32[4,128,128]{2,1,0:T(8,128)S(1)}, f32[4,128,128]{2,1,0:T(8,128)S(1)}, u32[]{:S(2)}, u32[]{:S(2)}) collective-permute-start(f32[4,128,128]{2,1,0:T(8,128)S(1)} %broadcast_select_fusion.2), channel_id=1, source_target_pairs={{16,0},{32,16},{48,32},{64,48},{80,64},{96,80},{112,96},{128,112},... | collective-permute-start | bytes 786440 | tf_op jit(solution)/shard_map/while/body/eval_jaxpr/ppermute | solution.py:29
  283.6 8.4 collective-permute-start.1
  290.6 9.8 %collective-permute-start.2 = (f32[1,128,128]{2,1,0:T(8,128)}, f32[1,128,128]{2,1,0:T(8,128)}, u32[]{:S(2)}, u32[]{:S(2)}) collective-permute-start(f32[1,128,128]{2,1,0:T(8,128)} %get-tuple-element.304), channel_id=1, source_target_pairs={{1,0},{2,1},{3,2},{4,3},{5,4},{6,5},{7,6},{8,7},{9,8},{10,9},{11,1... | collective-permute-start | bytes 196616 | tf_op jit(solution)/shard_map/while/body/eval_jaxpr/ppermute | solution.py:21
  314.2 8.9 collective-permute-start.1
  321.5 10.0 %collective-permute-start.2 = (f32[1,128,128]{2,1,0:T(8,128)}, f32[1,128,128]{2,1,0:T(8,128)}, u32[]{:S(2)}, u32[]{:S(2)}) collective-permute-start(f32[1,128,128]{2,1,0:T(8,128)} %get-tuple-element.304), channel_id=1, source_target_pairs={{1,0},{2,1},{3,2},{4,3},{5,4},{6,5},{7,6},{8,7},{9,8},{10,9},{11,1... | collective-permute-start | bytes 196616 | tf_op jit(solution)/shard_map/while/body/eval_jaxpr/ppermute | solution.py:21
  464.6 9.1 collective-permute-start
  490.5 9.3 %collective-permute-start = (f32[4,128,128]{2,1,0:T(8,128)S(1)}, f32[4,128,128]{2,1,0:T(8,128)S(1)}, u32[]{:S(2)}, u32[]{:S(2)}) collective-permute-start(f32[4,128,128]{2,1,0:T(8,128)S(1)} %broadcast_select_fusion.2), channel_id=1, source_target_pairs={{16,0},{32,16},{48,32},{64,48},{80,64},{96,80},{112,96},{128,112},... | collective-permute-start | bytes 786440 | tf_op jit(solution)/shard_map/while/body/eval_jaxpr/ppermute | solution.py:29
  516.3 9.1 %collective-permute-start = (f32[4,128,128]{2,1,0:T(8,128)S(1)}, f32[4,128,128]{2,1,0:T(8,128)S(1)}, u32[]{:S(2)}, u32[]{:S(2)}) collective-permute-start(f32[4,128,128]{2,1,0:T(8,128)S(1)} %broadcast_select_fusion.2), channel_id=1, source_target_pairs={{16,0},{32,16},{48,32},{64,48},{80,64},{96,80},{112,96},{128,112},... | collective-permute-start | bytes 786440 | tf_op jit(solution)/shard_map/while/body/eval_jaxpr/ppermute | solution.py:29
  541.9 9.4 %collective-permute-start = (f32[4,128,128]{2,1,0:T(8,128)S(1)}, f32[4,128,128]{2,1,0:T(8,128)S(1)}, u32[]{:S(2)}, u32[]{:S(2)}) collective-permute-start(f32[4,128,128]{2,1,0:T(8,128)S(1)} %broadcast_select_fusion.2), channel_id=1, source_target_pairs={{16,0},{32,16},{48,32},{64,48},{80,64},{96,80},{112,96},{128,112},... | collective-permute-start | bytes 786440 | tf_op jit(solution)/shard_map/while/body/eval_jaxpr/ppermute | solution.py:29
  568.2 9.3 %collective-permute-start = (f32[4,128,128]{2,1,0:T(8,128)S(1)}, f32[4,128,128]{2,1,0:T(8,128)S(1)}, u32[]{:S(2)}, u32[]{:S(2)}) collective-permute-start(f32[4,128,128]{2,1,0:T(8,128)S(1)} %broadcast_select_fusion.2), channel_id=1, source_target_pairs={{16,0},{32,16},{48,32},{64,48},{80,64},{96,80},{112,96},{128,112},... | collective-permute-start | bytes 786440 | tf_op jit(solution)/shard_map/while/body/eval_jaxpr/ppermute | solution.py:29
  594.3 9.7 %collective-permute-start = (f32[4,128,128]{2,1,0:T(8,128)S(1)}, f32[4,128,128]{2,1,0:T(8,128)S(1)}, u32[]{:S(2)}, u32[]{:S(2)}) collective-permute-start(f32[4,128,128]{2,1,0:T(8,128)S(1)} %broadcast_select_fusion.2), channel_id=1, source_target_pairs={{16,0},{32,16},{48,32},{64,48},{80,64},{96,80},{112,96},{128,112},... | collective-permute-start | bytes 786440 | tf_op jit(solution)/shard_map/while/body/eval_jaxpr/ppermute | solution.py:29
  620.3 8.7 collective-permute-start
  645.8 8.9 collective-permute-start
  671.7 8.6 collective-permute-start
  698.1 9.3 %collective-permute-start.38 = (f32[1,4,128,128]{2,3,1,0:T(8,128)S(1)}, f32[1,4,128,128]{2,3,1,0:T(8,128)S(1)}, u32[]{:S(2)}, u32[]{:S(2)}) collective-permute-start(f32[1,4,128,128]{2,3,1,0:T(8,128)S(1)} %copy.37), channel_id=1, source_target_pairs={{16,0},{32,16},{48,32},{64,48},{80,64},{96,80},{112,96},{128,112},... | collective-permute-start | bytes 786440 | tf_op jit(solution)/shard_map/ppermute | solution.py:29
  (266 other events, 2338.3 us)
Sparse Core Ops, SparseCore 0:
  826.5 78.4 reduce-scatter.1
where the time goes:
time: 930 us; the launch traced here: 912 us
  starting transfers between devices  357 us (38%)
  waiting for transfers between devices  296 us (32%)
  other arithmetic  179 us (19%)
  local copies, waits for them, and re-layouts  62.2 us (7%)
  between operations  16.4 us (2%)
    ppermute x41, starting transfers between devices, with_halo(): before = lax.ppermute(last, axis, up)  226 us
    ppermute x41, waiting for transfers between devices, with_halo(): after = lax.ppermute(first, axis, down)  115 us
    ppermute x18, waiting for transfers between devices, shifted(): return lax.ppermute(block, axis, route)  83.3 us
    reduce_scatter x1, waiting for transfers between devices, on_device(): sensitivity = lax.psum_scatter(total, 'tm', scatter_dimension=2, tiled=True)  78.6 us
    ppermute x18, starting transfers between devices, shifted(): return lax.ppermute(block, axis, route)  77.9 us
    ppermute x41, starting transfers between devices, with_halo(): after = lax.ppermute(first, axis, down)  52.8 us
    add x7, other arithmetic, on_device(): latest = stepped + weight * temps[offset][:, 1:-1]  44.7 us
    add x7, other arithmetic, on_device(): latest = stepped + weight * heat  42.7 us
  transfers between devices with their start and end apart: 101, of which 58 were waited for; matrix products, arithmetic and copies ran while one was open for 2% of the time, Pallas kernels for 0%

commit v1 on v0

v1 whole, which is shorter than its diff:
```python
import functools

import jax
import jax.numpy as jnp
from jax import lax
from jax.experimental import pallas as pl
from jax.experimental.pallas import tpu as pltpu
from jax.sharding import PartitionSpec as P

MESH = pl.DeviceIdType.MESH
F32 = jnp.float32

RATE = 0.006
SLOPE = 0.5
LEVELS = 8
Q, PLANES, ROWS, LANES = 4, 8, 16, 128
PADP, PADR = PLANES + 2, 32
MID_P = pl.ds(1, PLANES)
MID_R = pl.ds(8, ROWS)
XM, XP, YM, YP = range(4)


def kernel(
    ck, guess, mats, table, weight,
    out, sens_out,
    st, yh, ys, coef, base_src, bb, by, bp, kb, g, wt, res, cor, err, ey, ep, total, turned, sr, s2, sf,
    barrier_pad,
    ck_send, ck_recv, gu_send, gu_recv, bs_send, bs_recv, wt_send, wt_recv,
    bx_send, bx_recv, ex_send, ex_recv, hop_send, hop_recv, ch_send, ch_recv,
    ce_send, ce_recv, co_send, co_recv, r1_send, r1_recv, r2_send, r2_recv,
):
    t, s = lax.axis_index("tm"), lax.axis_index("space")
    y, zl, c = t // 4, (t // 2) % 2, t % 2
    x, zh = s // 4, s % 4
    z = zh * 2 + zl
    px = x * 2 + c
    mine = zl * 2 + c
    half = zh % 2

    def dev(px_, y_, z_):
        return {"tm": y_ * 4 + (z_ % 2) * 2 + px_ % 2, "space": (px_ // 2) * 4 + z_ // 2}

    near = [
        (px > 0, px - 1, z),
        (px < 7, px + 1, z),
        (z > 0, px, z - 1),
        (z < 7, px, z + 1),
    ]

    barrier = pltpu.get_barrier_semaphore()

    def greet(px_, y_, z_):
        pl.semaphore_signal(barrier, inc=1, device_id=dev(px_, y_, z_), device_id_type=MESH)

    def ring(i, count):
        z_, px_ = i // 2, x * 2 + i % 2
        other = jnp.logical_or(z_ != z, px_ != px)

        @pl.when(other)
        def _():
            greet(px_, y, z_)

        return count

    lax.fori_loop(0, 16, ring, 0)
    count = jnp.int32(15)
    far_ok = jnp.where(c == 0, px > 0, px < 7)
    far = jnp.where(c == 0, px - 1, px + 1)

    @pl.when(far_ok)
    def _():
        greet(far, y, z)

    count = count + far_ok.astype(jnp.int32)

    for dy in range(1, 4):
        y_ = (y + dy) % 4
        greet(px, y_, z)
    count = count + 3
    for dy in (-1, 1):
        y_ok = jnp.logical_and(y + dy >= 0, y + dy < 4)
        for ok, px_, z_ in near:
            both = jnp.logical_and(ok, y_ok)

            @pl.when(both)
            def _(px_=px_, z_=z_, dy=dy):
                greet(px_, y + dy, z_)

            count = count + both.astype(jnp.int32)

    def lookup(p, carry):
        ids = mats[p]
        val = jnp.zeros(ids.shape, F32)
        for number in range(8):
            val = val + jnp.where(ids == number, table[number], 0.0)
        base_src[p] = val
        return carry

    lax.fori_loop(0, 4, lookup, 0)

    row_zero = jnp.zeros((ROWS, LANES), F32)
    for side, plane in ((XM, 0), (XP, PADP - 1)):

        @pl.when(jnp.logical_not(near[side][0]))
        def _(plane=plane):
            bb[plane, MID_R] = row_zero
            for i in range(4):
                err[i, plane, MID_R] = row_zero

            def clear(i, carry):
                for q in range(Q):
                    st[i, q, plane, MID_R] = row_zero
                return carry

            lax.fori_loop(0, 3 * LEVELS, clear, 0)

    for side, k in ((YM, 0), (YP, 1)):

        @pl.when(jnp.logical_not(near[side][0]))
        def _(k=k):
            by[k] = jnp.zeros((PLANES, LANES), F32)
            for i in range(4):
                ey[i, k] = jnp.zeros((PLANES, LANES), F32)

            def clear(i, carry):
                yh[i, k] = jnp.zeros((Q * PLANES, LANES), F32)
                return carry

            lax.fori_loop(0, 3 * LEVELS, clear, 0)

    @pl.when(y == 3)
    def _():
        err[0] = jnp.zeros((PADP, PADR, LANES), F32)
        for k in range(2):
            ey[0, k] = jnp.zeros((PLANES, LANES), F32)
        st[LEVELS, 3, MID_P, MID_R] = jnp.zeros((PLANES, ROWS, LANES), F32)

    pl.semaphore_wait(barrier, count)

    def push(src, dst, ssem, rsem, px_, y_, z_):
        here = jnp.logical_and(jnp.logical_and(px_ == px, z_ == z), y_ == y)

        @pl.when(here)
        def _():
            pltpu.make_async_copy(src, dst, rsem).start()

        @pl.when(jnp.logical_not(here))
        def _():
            pltpu.make_async_remote_copy(
                src_ref=src, dst_ref=dst, send_sem=ssem, recv_sem=rsem,
                device_id=dev(px_, y_, z_), device_id_type=MESH,
            ).start()

    def push_done(src, ssem, px_, y_, z_):
        here = jnp.logical_and(jnp.logical_and(px_ == px, z_ == z), y_ == y)

        @pl.when(jnp.logical_not(here))
        def _():
            pltpu.make_async_copy(src, src, ssem).wait()

    def arrived(dst, rsem):
        pltpu.make_async_copy(dst, dst, rsem).wait()

    to_px = x * 2 + zh // 2
    slot = half * 4 + mine

    def cut(ref, z_):
        return ref.at[pl.ds(0, 4), pl.ds(pl.multiple_of(z_ * ROWS, ROWS), ROWS)]

    def send_ck(i, carry):
        z_ = (z + i) % 8
        push(cut(ck.at[0], z_), st.at[0, mine, pl.ds(1 + 4 * half, 4), MID_R], ck_send.at[i], ck_recv.at[slot], to_px, y, z_)
        return carry

    def send_guess(i, carry):
        z_ = (z + i) % 8
        push(cut(guess.at[0], z_), g.at[mine, pl.ds(4 * half, 4)], gu_send.at[i], gu_recv.at[slot], to_px, y, z_)
        return carry

    for i in range(2):
        z_ = 2 * mine + i
        push(cut(base_src, z_), bb.at[pl.ds(1 + 4 * half, 4), MID_R], bs_send.at[i], bs_recv.at[half], to_px, y, z_)
    lax.fori_loop(0, 8, send_ck, 0)
    for i in range(2):
        z_ = 2 * mine + i
        push(cut(weight, z_), wt.at[pl.ds(4 * half, 4)], wt_send.at[i], wt_recv.at[half], to_px, y, z_)

    def faces(plane_src, row_src, plane_dst, row_dst, ssem, rsem, y_, start, wait):
        sides = [
            (XM, plane_src(1), plane_dst(PADP - 1), XP),
            (XP, plane_src(PLANES), plane_dst(0), XM),
            (YM, row_src(0), row_dst(1), YP),
            (YP, row_src(1), row_dst(0), YM),
        ]
        for side, src, dst, lands in sides:
            ok, px_, z_ = near[side]

            @pl.when(ok)
            def _(side=side, src=src, dst=dst, lands=lands, px_=px_, z_=z_):
                copy = pltpu.make_async_remote_copy(
                    src_ref=src, dst_ref=dst, send_sem=ssem(side), recv_sem=rsem(lands),
                    device_id=dev(px_, y_, z_), device_id_type=MESH,
                )
                if start:
                    copy.start()
                if wait:
                    copy.wait_send()

    def landed(plane_dst, row_dst, rsem):
        sides = [(XM, plane_dst(0)), (XP, plane_dst(PADP - 1)), (YM, row_dst(0)), (YP, row_dst(1))]
        for side, dst in sides:

            @pl.when(near[side][0])
            def _(side=side, dst=dst):
                arrived(dst, rsem(side))

    def batch_args(idx, phase):
        par = idx % 2
        plane = lambda p: st.at[idx, pl.ds(0, Q), p, MID_R]
        return (
            plane, lambda k: ys.at[idx, k], plane, lambda k: yh.at[idx, k],
            lambda side: ex_send.at[phase, par, side], lambda side: ex_recv.at[phase, par, side],
        )

    def batch_start(idx, phase):
        def pack(q, carry):
            for k, row in ((0, 8), (1, 8 + ROWS - 1)):
                for p in range(PLANES):
                    ys[idx, k, pl.ds(q * PLANES + p, 1)] = st[idx, q, 1 + p, pl.ds(row, 1)]
            return carry

        lax.fori_loop(0, Q, pack, 0)
        ps, rs, pd, rd, ss, rr = batch_args(idx, phase)
        faces(ps, rs, pd, rd, ss, rr, y, True, False)

    def batch_wait(idx, phase):
        ps, rs, pd, rd, ss, rr = batch_args(idx, phase)
        landed(pd, rd, rr)
        faces(ps, rs, pd, rd, ss, rr, y, False, True)

        def unpack(q, carry):
            for k, row in ((0, 7), (1, 8 + ROWS)):
                for p in range(PLANES):
                    st[idx, q, 1 + p, pl.ds(row, 1)] = yh[idx, k, pl.ds(q * PLANES + p, 1)]
            return carry

        lax.fori_loop(0, Q, unpack, 0)

    for i in range(2):
        arrived(bb.at[pl.ds(1 + 4 * i, 4), MID_R], bs_recv.at[i])
    for p in range(PLANES):
        for k, row in ((0, 8), (1, 8 + ROWS - 1)):
            bp[k, pl.ds(p, 1)] = bb[1 + p, pl.ds(row, 1)]
    base_plane = lambda p: bb.at[p, MID_R]
    base_args = (
        base_plane, lambda k: bp.at[k], base_plane, lambda k: by.at[k],
        lambda side: bx_send.at[side], lambda side: bx_recv.at[side],
    )
    faces(*base_args, y, True, False)

    for i in range(8):
        arrived(st.at[0, i % 4, pl.ds(1 + 4 * (i // 4), 4), MID_R], ck_recv.at[i])
    batch_start(0, 0)

    landed(base_args[2], base_args[3], base_args[5])
    faces(*base_args, y, False, True)
    for p in range(PLANES):
        for k, row in ((0, 7), (1, 8 + ROWS)):
            bb[1 + p, pl.ds(row, 1)] = by[k, pl.ds(p, 1)]
    for i in range(2):
        arrived(wt.at[pl.ds(4 * i, 4)], wt_recv.at[i])

    lane = lax.broadcasted_iota(jnp.int32, (PLANES, ROWS, LANES), 2)
    first, last = lane == 0, lane == LANES - 1

    def beside(ref):
        mid = ref[MID_P, MID_R]
        return mid, [
            ref[pl.ds(0, PLANES), MID_R],
            ref[pl.ds(2, PLANES), MID_R],
            ref[MID_P, pl.ds(7, ROWS)],
            ref[MID_P, pl.ds(9, ROWS)],
            pltpu.roll(mid, 1, 2),
            pltpu.roll(mid, LANES - 1, 2),
        ]

    def clipped(around):
        return around[:4] + [jnp.where(first, 0.0, around[4]), jnp.where(last, 0.0, around[5])]

    def conductivity(j):
        def one(q, carry):
            kb[q] = bb[...] * (1.0 + SLOPE * st[j, q])
            return carry

        lax.fori_loop(0, Q, one, 0)

    def forward(j):
        def one(q, carry):
            u, u_d = beside(st.at[j, q])
            k, k_d = beside(kb.at[q])
            flow = jnp.zeros_like(u)
            for uu, kk in zip(clipped(u_d), clipped(k_d)):
                flow = flow + (k + kk) * (uu - u)
            st[j + 1, q, MID_P, MID_R] = u + (0.5 * RATE) * flow
            return carry

        lax.fori_loop(0, Q, one, 0)

    def coefficients(j):
        def one(q, carry):
            u, u_d = beside(st.at[j, q])
            k, k_d = beside(kb.at[q])
            b = (0.25 * SLOPE * 2.0 * RATE) * bb[MID_P, MID_R]
            gain = (0.5 * RATE) * (1.0 + SLOPE * u)
            w_sum = jnp.zeros_like(u)
            e_sum = jnp.zeros_like(u)
            for n, (uu, kk) in enumerate(zip(clipped(u_d), clipped(k_d))):
                diff = uu - u
                w = (0.5 * RATE) * (k + kk) - b * diff
                e = gain * diff
                w_sum = w_sum + w
                e_sum = e_sum + e
                if n == 4:
                    w, e = jnp.where(first, 0.0, w), jnp.where(first, 0.0, e)
                if n == 5:
                    w, e = jnp.where(last, 0.0, w), jnp.where(last, 0.0, e)
                coef[j, q, 1 + n] = w
                coef[j, q, 8 + n] = e
            coef[j, q, 0] = w_sum
            coef[j, q, 7] = e_sum
            coef[j, q, 14] = wt[...] * u
            return carry

        lax.fori_loop(0, Q, one, 0)

    def hop_copy():
        return pltpu.make_async_remote_copy(
            src_ref=g.at[0], dst_ref=st.at[LEVELS, 3, MID_P, MID_R], send_sem=hop_send, recv_sem=hop_recv,
            device_id=dev(px, (y + 3) % 4, z), device_id_type=MESH,
        )

    def forward_step(j, carry):
        batch_wait(j, 0)
        conductivity(j)

        @pl.when(j < LEVELS - 1)
        def _():
            forward(j)
            batch_start(j + 1, 0)

        @pl.when(j < 4)
        def _():
            send_guess(2 * j, 0)
            send_guess(2 * j + 1, 0)

        @pl.when(j == 5)
        def _():
            for i in range(8):
                arrived(g.at[i % 4, pl.ds(4 * (i // 4), 4)], gu_recv.at[i])

            @pl.when(y > 0)
            def _():
                hop_copy().start()

            for q in range(3):
                st[LEVELS, q, MID_P, MID_R] = g[q + 1]

        @pl.when(j == LEVELS - 1)
        def _():
            @pl.when(y < 3)
            def _():
                hop_copy().wait_recv()

            batch_start(LEVELS, 1)

        coefficients(j)
        return carry

    lax.fori_loop(0, LEVELS, forward_step, 0)

    def apply(ref, j, q, at):
        v, v_d = beside(ref)
        acc = v_d[0] * coef[j, q, at + 1]
        for n in range(1, 6):
            acc = acc + v_d[n] * coef[j, q, at + 1 + n]
        return v, acc - v * coef[j, q, at]

    def adjoint(idx, j):
        def one(q, carry):
            v, change = apply(st.at[idx, q], j, q, 0)
            st[idx + 1, q, MID_P, MID_R] = (v + change) + coef[j, q, 14]
            return carry

        lax.fori_loop(0, Q, one, 0)

    def relax_step(i, carry):
        idx = LEVELS + i
        batch_wait(idx, 1)
        adjoint(idx, LEVELS - 1 - i)

        @pl.when(i < LEVELS - 1)
        def _():
            batch_start(idx + 1, 1)

        return carry

    lax.fori_loop(0, LEVELS, relax_step, 0)

    def residual(q, carry):
        res[q] = st[2 * LEVELS, q, MID_P, MID_R] - g[q]
        return carry

    lax.fori_loop(0, Q, residual, 0)

    def err_args(i, ssem, rsem, to=None):
        to = i if to is None else to
        return (
            lambda p: err.at[i, p, MID_R], lambda k: ep.at[i, k],
            lambda p: err.at[to, p, MID_R], lambda k: ey.at[to, k], ssem, rsem,
        )

    def err_pack(i):
        for p in range(PLANES):
            for k, row in ((0, 8), (1, 8 + ROWS - 1)):
                ep[i, k, pl.ds(p, 1)] = err[i, 1 + p, pl.ds(row, 1)]

    def err_unpack(i):
        for p in range(PLANES):
            for k, row in ((0, 7), (1, 8 + ROWS)):
                err[i, 1 + p, pl.ds(row, 1)] = ey[i, k, pl.ds(p, 1)]

    def cross_args():
        return err_args(4, lambda side: ce_send.at[side], lambda side: ce_recv.at[side], to=0)

    def block_copy():
        return pltpu.make_async_remote_copy(
            src_ref=err.at[4, MID_P, MID_R], dst_ref=err.at[0, MID_P, MID_R], send_sem=ce_send.at[4], recv_sem=ce_recv.at[4],
            device_id=dev(px, (y + 3) % 4, z), device_id_type=MESH,
        )

    def give(q, i, start):
        src = cor.at[q, pl.ds(4 * i, 4)]
        z_, px_ = 2 * (2 * c + i) + q // 2, x * 2 + q % 2
        if start:
            push(src, out.at[0, pl.ds(0, 4), pl.ds(pl.multiple_of(z * ROWS, ROWS), ROWS)], co_send.at[q, i], co_recv.at[z], px_, y, z_)
        else:
            push_done(src, co_send.at[q, i], px_, y, z_)

    for i in range(4):
        q = 3 - i
        if i == 0:

            @pl.when(y < 3)
            def _():
                a = cross_args()
                landed(a[2], a[3], a[5])
                block_copy().wait_recv()

        else:
            a = err_args(i, lambda side, i=i: ch_send.at[i - 1, side], lambda side, i=i: ch_recv.at[i - 1, side])
            landed(a[2], a[3], a[5])
            faces(*a, y, False, True)
        err_unpack(i)
        e, change = apply(err.at[i], 0, q, 0)
        err[i + 1, MID_P, MID_R] = (e + float(LEVELS) * change) + res[q]
        err_pack(i + 1)
        if i < 3:
            a = err_args(i + 1, lambda side, i=i: ch_send.at[i, side], lambda side, i=i: ch_recv.at[i, side])
            faces(*a, y, True, False)
        else:

            @pl.when(y > 0)
            def _():
                block_copy().start()
                faces(*cross_args(), y - 1, True, False)

        st[2 * LEVELS, q] = st[LEVELS, q] + err[i]
        cor[q] = g[q] + err[i + 1, MID_P, MID_R]
        for k in range(2):
            give(q, k, True)

    total[...] = jnp.zeros(total.shape, F32)

    def final_step(i, carry):
        idx = 2 * LEVELS + i
        j = LEVELS - 1 - i

        @pl.when(i > 0)
        def _():
            batch_wait(idx, 2)

        @pl.when(i < LEVELS - 1)
        def _():
            adjoint(idx, j)
            batch_start(idx + 1, 2)

        def one(q, carry):
            _, change = apply(st.at[idx, q], j, q, 7)
            total[...] = total[...] - change
            return carry

        lax.fori_loop(0, Q, one, 0)
        return carry

    lax.fori_loop(0, LEVELS, final_step, 0)

    turned[...] = jnp.transpose(total[...].reshape(PLANES * ROWS, LANES))

    def sum_copy(dy):
        y_ = (y + dy) % 4
        src = turned.at[pl.ds(pl.multiple_of(y_ * 32, 32), 32)]
        return pltpu.make_async_remote_copy(
            src_ref=src, dst_ref=sr.at[dy - 1], send_sem=r1_send.at[dy - 1], recv_sem=r1_recv.at[dy - 1],
            device_id=dev(px, y_, z), device_id_type=MESH,
        )

    for dy in range(1, 4):
        sum_copy(dy).start()
    part = turned[pl.ds(pl.multiple_of(y * 32, 32), 32)]
    for dy in range(1, 4):
        sum_copy(dy).wait_recv()
        part = part + sr[dy - 1]
    s2[0] = part
    s2[1] = pltpu.roll(part, 64, 1)

    def share(n, start):
        i, q = n // 4, n % 4
        src = s2.at[i, pl.ds(8 * q, 8)]
        z_, px_ = 2 * (2 * c + i) + q // 2, x * 2 + q % 2
        if start:
            push(src, sf.at[z], r2_send.at[n], r2_recv.at[z], px_, y, z_)
        else:
            push_done(src, r2_send.at[n], px_, y, z_)

    for n in range(8):
        share(n, True)
    for i in range(8):
        arrived(sf.at[i], r2_recv.at[i])
    sens_out[...] = sf[...]

    for n in range(8):
        share(n, False)
    for dy in range(1, 4):
        sum_copy(dy).wait_send()
    for q in range(4):
        for i in range(2):
            give(q, i, False)
    for i in range(8):
        arrived(out.at[0, pl.ds(0, 4), pl.ds(i * ROWS, ROWS)], co_recv.at[i])

    @pl.when(y > 0)
    def _():
        hop_copy().wait_send()
        block_copy().wait_send()
        faces(*cross_args(), y - 1, False, True)

    for i in range(2):
        z_ = 2 * mine + i
        push_done(cut(base_src, z_), bs_send.at[i], to_px, y, z_)
        push_done(cut(weight, z_), wt_send.at[i], to_px, y, z_)

    def drain(i, carry):
        z_ = (z + i) % 8
        push_done(cut(ck.at[0], z_), ck_send.at[i], to_px, y, z_)
        push_done(cut(guess.at[0], z_), gu_send.at[i], to_px, y, z_)
        return carry

    lax.fori_loop(0, 8, drain, 0)


def on_device(checkpoints, guess, materials, table, weight):
    dma = pltpu.SemaphoreType.DMA
    vmem = lambda *shape: pltpu.VMEM(shape, F32)
    block = (PLANES, ROWS, LANES)
    corrected, shares = pl.pallas_call(
        kernel,
        out_shape=(
            jax.ShapeDtypeStruct(guess.shape, F32),
            jax.ShapeDtypeStruct((8, 8, LANES), F32),
        ),
        in_specs=[
            pl.BlockSpec(memory_space=pl.ANY),
            pl.BlockSpec(memory_space=pl.ANY),
            pl.BlockSpec(memory_space=pltpu.VMEM),
            pl.BlockSpec(memory_space=pltpu.SMEM),
            pl.BlockSpec(memory_space=pl.ANY),
        ],
        out_specs=(
            pl.BlockSpec(memory_space=pl.ANY),
            pl.BlockSpec(memory_space=pltpu.VMEM),
        ),
        scratch_shapes=[
            vmem(3 * LEVELS, Q, PADP, PADR, LANES),
            vmem(3 * LEVELS, 2, Q * PLANES, LANES),
            vmem(3 * LEVELS, 2, Q * PLANES, LANES),
            vmem(LEVELS, Q, 15, *block),
            vmem(4, 128, LANES),
            vmem(PADP, PADR, LANES),
            vmem(2, PLANES, LANES),
            vmem(2, PLANES, LANES),
            vmem(Q, PADP, PADR, LANES),
            vmem(Q, *block),
            vmem(*block),
            vmem(Q, *block),
            vmem(Q, *block),
            vmem(5, PADP, PADR, LANES),
            vmem(5, 2, PLANES, LANES),
            vmem(5, 2, PLANES, LANES),
            vmem(*block),
            vmem(LANES, LANES),
            vmem(3, 32, LANES),
            vmem(2, 32, LANES),
            vmem(8, 8, LANES),
            vmem(8, LANES),
            dma((8,)), dma((8,)), dma((8,)), dma((8,)),
            dma((2,)), dma((2,)), dma((2,)), dma((2,)),
            dma((4,)), dma((4,)),
            dma((3, 2, 4)), dma((3, 2, 4)),
            dma, dma,
            dma((3, 4)), dma((3, 4)),
            dma((5,)), dma((5,)),
            dma((4, 2)), dma((8,)),
            dma((3,)), dma((3,)), dma((8,)), dma((8,)),
        ],
        compiler_params=pltpu.CompilerParams(
            collective_id=0, has_side_effects=True, vmem_limit_bytes=60 * 1024 * 1024
        ),
    )(checkpoints, guess, materials, table, weight)
    parts = shares[:, :, :64].reshape(8, 8, 4, 16)
    sensitivity = jnp.transpose(parts, (2, 0, 3, 1)).reshape(4, 128, 8)
    return corrected, sensitivity


def solution(mesh):
    in_specs = (
        P("tm", "space", None, None),
        P("tm", "space", None, None),
        P("space", None, None),
        P(),
        P("space", None, None),
    )
    out_specs = (P("tm", "space", None, None), P("space", None, "tm"))
    return jax.shard_map(
        on_device, mesh=mesh, in_specs=in_specs, out_specs=out_specs, check_vma=False
    )
```

time: 930 us -> 179 us (0.19); the launches traced: 912 us -> 178 us
  starting transfers between devices: 357 us -> 0 us
  waiting for transfers between devices: 296 us -> 0 us
  other arithmetic: 179 us -> 0 us
  Pallas kernels: 0 us -> 175 us
  local copies, waits for them, and re-layouts: 62.2 us -> 2.41 us
  between operations: 16.4 us -> 0.66 us
    ppermute x100 -> x0, starting transfers between devices: 357 us -> none  [the longest x41 226 us: with_halo(): before = lax.ppermute(last, axis, up)]
    ppermute x100 -> x0, waiting for transfers between devices: 217 us -> none  [the longest x41 115 us: with_halo(): after = lax.ppermute(first, axis, down)]
    pallas_call x0 -> x1, Pallas kernels: none -> 175 us  [on_device(): pl.pallas_call(kernel, out_shape=(jax.ShapeDtypeStruct(guess.shape, F32),...]
    add x40 -> x0, other arithmetic: 137 us -> none  [the longest x7 44.7 us: on_device(): latest = stepped + weight * temps[offset][:, 1:-1]]
    reduce_scatter x1 -> x0, waiting for transfers between devices: 78.6 us -> none  [on_device(): sensitivity = lax.psum_scatter(total, 'tm', scatter_dimension=2, tiled=True)]
    concatenate x35 -> x0, other arithmetic: 32.2 us -> none  [with_halo(): shard = jnp.concatenate([before, shard, after], axis=dim)]
    while x208 -> x0, local copies, waits for them, and re-layouts: 28.2 us -> none
    unnamed x212 -> x3, local copies, waits for them, and re-layouts: 18.6 us -> 0.71 us
  transfers between devices with their start and end apart: 101 -> 0, of which waited for: 58 -> 0; matrix products, arithmetic and copies ran while one was open for 2% -> 0% of each run, Pallas kernels for 0% -> 0%
where the time goes in v1:
time: 179 us; the launch traced here: 178 us
  Pallas kernels  175 us (98%)
  local copies, waits for them, and re-layouts  2.41 us (1%)
    pallas_call x1, Pallas kernels, on_device(): pl.pallas_call(kernel, out_shape=(jax.ShapeDtypeStruct(guess.shape, F32),...  175 us

profile of v1, /device:TPU:17, one launch (start us, length us, event | category | flops | bytes accessed | tf_op | source)
XLA Modules:
  0.0 178.4 jit_solution(12344134831422095076)
XLA Ops:
  0.6 175.3 %shard_map.68 = (f32[1,4,128,128]{3,2,1,0:T(8,128)}, f32[8,8,128]{2,1,0:T(8,128)}) custom-call(f32[1,4,128,128]{3,2,1,0:T(8,128)} %ck.1, f32[1,4,128,128]{3,2,1,0:T(8,128)} %guess.1, s32[4,128,128]{2,1,0:T(8,128)} %mats.1, f32[8]{0:T(128)} %table.1, f32[4,128,128]{2,1,0:T(8,128)} %weight.1), custom_call_target="tpu_custom_call" | custom-call | tf_op jit(solution)/shard_map/pallas_call | solution.py:575
  176.0 0.0 copy-start
  176.0 0.9 reshape.10
  176.9 0.1 copy.7
  177.0 0.7 reshape.11
  177.7 0.0 copy-done
  177.7 0.7 copy.9
Async XLA Ops:
  176.0 1.7 copy-start

commit v2 on v1

v2 whole, which is shorter than its diff:
```python
import functools

import jax
import jax.numpy as jnp
from jax import lax
from jax.experimental import pallas as pl
from jax.experimental.pallas import tpu as pltpu
from jax.sharding import PartitionSpec as P

MESH = pl.DeviceIdType.MESH
F32 = jnp.float32

RATE = 0.006
SLOPE = 0.5
LEVELS = 8
Q, PLANES, ROWS, LANES, H = 4, 8, 16, 128, 4
PADP, PADR = PLANES + 2 * H, ROWS + 2 * H
MID_P, MID_R = pl.ds(H, PLANES), pl.ds(H, ROWS)
SIDES = [(-1, 0), (1, 0), (0, -1), (0, 1), (-1, -1), (1, -1), (-1, 1), (1, 1)]
OPPOSITE = [SIDES.index((-dx, -dz)) for dx, dz in SIDES]
RELAX, FINAL, U2, U6 = 8, 9, 17, 18
EXCHANGED = [0, 3, 7, U2, U6, RELAX, RELAX + 4, RELAX + 8, FINAL, FINAL + 4]
WIDTH = [3, 1, 2, 3, 0, 1, 2, 3]
PLACE = [(3, 1), (2, 1), (1, 1), (0, 1), (3, 0), (2, 0), (1, 0), (0, 0)]
COEF_W = [3, 2, 1, 3]


def chunks(width):
    lo, hi = H - width, H + PLANES + width
    parts = -(-(hi - lo) // 5)
    edges = [lo + (hi - lo) * n // parts for n in range(parts + 1)]
    return list(zip(edges[:-1], edges[1:]))


def kernel(
    ck, guess, mats, table, weight,
    out, sens_out,
    st, yh, ys, c0, c1, c2, c3, base_src, cin, bin_, win, bb, wt, bwh, bws, g, gn, g0, cor, err, ei, eo, eyh, eys,
    total, turned, sr, s2, sf,
    ck_send, ck_recv, gu_send, gu_recv, bs_send, bs_recv, wt_send, wt_recv,
    bx_send, bx_recv, ex_send, ex_recv, hop_send, hop_recv,
    ce_send, ce_recv, co_send, co_recv, r1_send, r1_recv, r2_send, r2_recv,
):
    coef = [c0, c1, c2, c3]
    t, s = lax.axis_index("tm"), lax.axis_index("space")
    y, zl, c = t // 4, (t // 2) % 2, t % 2
    x, zh = s // 4, s % 4
    z = zh * 2 + zl
    px = x * 2 + c
    mine = zl * 2 + c
    half = zh % 2

    def dev(px_, y_, z_):
        return {"tm": y_ * 4 + (z_ % 2) * 2 + px_ % 2, "space": (px_ // 2) * 4 + z_ // 2}

    def there(dx, dz):
        ok = jnp.bool_(True)
        if dx:
            ok = px > 0 if dx < 0 else px < 7
        if dz:
            ok_z = z > 0 if dz < 0 else z < 7
            ok = jnp.logical_and(ok, ok_z) if dx else ok_z
        return ok

    near = [(there(dx, dz), px + dx, z + dz) for dx, dz in SIDES]

    barrier = pltpu.get_barrier_semaphore()

    def greet(px_, y_, z_):
        pl.semaphore_signal(barrier, inc=1, device_id=dev(px_, y_, z_), device_id_type=MESH)

    def ring(i, carry):
        z_, px_ = i // 2, x * 2 + i % 2

        @pl.when(jnp.logical_or(z_ != z, px_ != px))
        def _():
            greet(px_, y, z_)

        return carry

    lax.fori_loop(0, 16, ring, 0)
    count = jnp.int32(15)
    far_ok = jnp.where(c == 0, px > 0, px < 7)
    far = jnp.where(c == 0, px - 1, px + 1)
    for dz in (-1, 0, 1):
        ok = jnp.logical_and(far_ok, there(0, dz)) if dz else far_ok

        @pl.when(ok)
        def _(dz=dz):
            greet(far, y, z + dz)

        count = count + ok.astype(jnp.int32)

    for dy in range(1, 4):
        greet(px, (y + dy) % 4, z)
    count = count + 3
    for dy in (-1, 1):
        y_ok = jnp.logical_and(y + dy >= 0, y + dy < 4)
        for ok, px_, z_ in near:
            both = jnp.logical_and(ok, y_ok)

            @pl.when(both)
            def _(px_=px_, z_=z_, dy=dy):
                greet(px_, y + dy, z_)

            count = count + both.astype(jnp.int32)

    def lookup(p, carry):
        ids = mats[p]
        val = jnp.zeros(ids.shape, F32)
        for number in range(8):
            val = val + jnp.where(ids == number, table[number], 0.0)
        base_src[p] = val
        return carry

    lax.fori_loop(0, 4, lookup, 0)

    for side, lo, rows in ((0, 0, 0), (1, H + PLANES, 48)):

        @pl.when(jnp.logical_not(near[side][0]))
        def _(lo=lo, rows=rows):
            slab = jnp.zeros((H, PADR, LANES), F32)
            for ref in (bb, wt, err.at[0]):
                ref[pl.ds(lo, H)] = slab
            edge = jnp.zeros((16, LANES), F32)
            for k in range(2):
                for n in range(2):
                    bwh[n, k, 0, pl.ds(rows, 16)] = edge
                eyh[k, 0, pl.ds(rows, 16)] = edge

            def clear(q, carry):
                for n, idx in enumerate(EXCHANGED):
                    st[idx, q, pl.ds(lo, H)] = slab
                    for k in range(2):
                        yh[n, k, q, pl.ds(rows, 16)] = edge
                return carry

            lax.fori_loop(0, Q, clear, 0)

    for side, k in ((2, 0), (3, 1)):

        @pl.when(jnp.logical_not(near[side][0]))
        def _(k=k):
            edge = jnp.zeros((64, LANES), F32)
            for n in range(2):
                bwh[n, k, 0] = edge
            eyh[k, 0] = edge

            def clear(q, carry):
                for n in range(len(EXCHANGED)):
                    yh[n, k, q] = edge
                return carry

            lax.fori_loop(0, Q, clear, 0)

    @pl.when(y == 3)
    def _():
        err[0] = jnp.zeros((PADP, PADR, LANES), F32)
        gn[...] = jnp.zeros(gn.shape, F32)

    pl.semaphore_wait(barrier, count)

    def push(src, dst, ssem, rsem, px_, y_, z_):
        here = jnp.logical_and(px_ == px, z_ == z)

        @pl.when(here)
        def _():
            pltpu.make_async_copy(src, dst, rsem).start()

        @pl.when(jnp.logical_not(here))
        def _():
            pltpu.make_async_remote_copy(
                src_ref=src, dst_ref=dst, send_sem=ssem, recv_sem=rsem,
                device_id=dev(px_, y_, z_), device_id_type=MESH,
            ).start()

    def push_done(src, ssem, px_, y_, z_):
        here = jnp.logical_and(px_ == px, z_ == z)

        @pl.when(jnp.logical_not(here))
        def _():
            pltpu.make_async_copy(src, src, ssem).wait()

    def arrived(dst, rsem):
        pltpu.make_async_copy(dst, dst, rsem).wait()

    to_px = x * 2 + zh // 2
    slot = half * 4 + mine

    def cut(ref, z_):
        return ref.at[pl.ds(0, 4), pl.ds(pl.multiple_of(z_ * ROWS, ROWS), ROWS)]

    def send_ck(i, carry):
        z_ = (z + i) % 8
        push(cut(ck.at[0], z_), cin.at[mine, pl.ds(4 * half, 4)], ck_send.at[i], ck_recv.at[slot], to_px, y, z_)
        return carry

    def send_guess(i, carry):
        z_ = (z + i) % 8
        push(cut(guess.at[0], z_), g.at[mine, pl.ds(4 * half, 4)], gu_send.at[i], gu_recv.at[slot], to_px, y, z_)
        return carry

    for i in range(2):
        z_ = 2 * mine + i
        push(cut(base_src, z_), bin_.at[pl.ds(4 * half, 4)], bs_send.at[i], bs_recv.at[half], to_px, y, z_)
    lax.fori_loop(0, 8, send_ck, 0)
    for i in range(2):
        z_ = 2 * mine + i
        push(cut(weight, z_), win.at[pl.ds(4 * half, 4)], wt_send.at[i], wt_recv.at[half], to_px, y, z_)

    def outgoing(field, side):
        planes, rows_out, _ = field
        dx, dz = SIDES[side]
        if dz == 0:
            return planes(H if dx < 0 else PLANES, H)
        k = 0 if dz < 0 else 1
        return rows_out(k, 16 if dx > 0 else 0, 32 if dx == 0 else 16)

    def landing(field, side):
        planes, _, rows_in = field
        dx, dz = SIDES[side]
        if dz == 0:
            return planes(0 if dx < 0 else H + PLANES, H)
        k = 0 if dz < 0 else 1
        return rows_in(k, {0: 16, -1: 0, 1: 48}[dx], 32 if dx == 0 else 16)

    def halo_copy(field, to, side, ssem, rsem, y_):
        _, px_, z_ = near[side]
        back = OPPOSITE[side]
        return pltpu.make_async_remote_copy(
            src_ref=outgoing(field, side), dst_ref=landing(to, back), send_sem=ssem(side), recv_sem=rsem(back),
            device_id=dev(px_, y_, z_), device_id_type=MESH,
        )

    def halo_start(field, to, ssem, rsem, y_):
        for side in (4, 5, 6, 7, 2, 3, 0, 1):

            @pl.when(near[side][0])
            def _(side=side):
                halo_copy(field, to, side, ssem, rsem, y_).start()

    def halo_sent(field, to, ssem, rsem, y_, sides=range(8)):
        for side in sides:

            @pl.when(near[side][0])
            def _(side=side):
                halo_copy(field, to, side, ssem, rsem, y_).wait_send()

    def halo_landed(field, rsem):
        for side in range(8):

            @pl.when(near[side][0])
            def _(side=side):
                arrived(landing(field, side), rsem(side))

    def pack(block, out_rows):
        for p in range(PLANES):
            out_rows[0, pl.ds(4 * p, 4)] = block[H + p, pl.ds(H, 4)]
            out_rows[1, pl.ds(4 * p, 4)] = block[H + p, pl.ds(ROWS, 4)]

    def unpack(block, in_rows):
        for p in range(PADP):
            block[p, pl.ds(0, 4)] = in_rows[0, pl.ds(4 * p, 4)]
            block[p, pl.ds(H + ROWS, 4)] = in_rows[1, pl.ds(4 * p, 4)]

    def batch(idx):
        n = EXCHANGED.index(idx)
        field = (
            lambda lo, m: st.at[idx, pl.ds(0, Q), pl.ds(lo, m)],
            lambda k, lo, m: ys.at[n, k, pl.ds(0, Q), pl.ds(lo, m)],
            lambda k, lo, m: yh.at[n, k, pl.ds(0, Q), pl.ds(lo, m)],
        )
        return n, field, lambda side: ex_send.at[n, side], lambda side: ex_recv.at[n, side]

    def per_q(one):
        def body(q, carry):
            one(q)
            return carry

        lax.fori_loop(0, Q, body, 0)

    def batch_start(idx):
        n, field, ssem, rsem = batch(idx)

        def one(q):
            for p in range(PLANES):
                ys[n, 0, q, pl.ds(4 * p, 4)] = st[idx, q, H + p, pl.ds(H, 4)]
                ys[n, 1, q, pl.ds(4 * p, 4)] = st[idx, q, H + p, pl.ds(ROWS, 4)]

        per_q(one)
        halo_start(field, field, ssem, rsem, y)

    def batch_wait(idx):
        n, field, ssem, rsem = batch(idx)
        halo_landed(field, rsem)
        halo_sent(field, field, ssem, rsem, y, (0, 1))

        def one(q):
            for p in range(PADP):
                st[idx, q, p, pl.ds(0, 4)] = yh[n, 0, q, pl.ds(4 * p, 4)]
                st[idx, q, p, pl.ds(H + ROWS, 4)] = yh[n, 1, q, pl.ds(4 * p, 4)]

        per_q(one)

    def batch_sent(idx):
        n, field, ssem, rsem = batch(idx)
        halo_sent(field, field, ssem, rsem, y, range(2, 8))

    def static_field(n):
        ref = bb if n == 0 else wt
        field = (
            lambda lo, m: ref.at[pl.ds(lo, m)],
            lambda k, lo, m: bws.at[n, k, 0, pl.ds(lo, m)],
            lambda k, lo, m: bwh.at[n, k, 0, pl.ds(lo, m)],
        )
        return field, lambda side: bx_send.at[n, side], lambda side: bx_recv.at[n, side]

    def static_start(n):
        ref, came, sem = (bb, bin_, bs_recv) if n == 0 else (wt, win, wt_recv)
        for i in range(2):
            arrived(came.at[pl.ds(4 * i, 4)], sem.at[i])
        ref[MID_P, MID_R] = came[...]
        pack(ref, bws.at[n, pl.ds(0, 2), 0])
        field, ssem, rsem = static_field(n)
        halo_start(field, field, ssem, rsem, y)

    def static_wait(n):
        field, ssem, rsem = static_field(n)
        halo_landed(field, rsem)
        halo_sent(field, field, ssem, rsem, y, (0, 1))
        unpack(bb if n == 0 else wt, bwh.at[n, pl.ds(0, 2), 0])

    static_start(0)
    for i in range(8):
        arrived(cin.at[i % 4, pl.ds(4 * (i // 4), 4)], ck_recv.at[i])

    def enter(q):
        st[0, q, MID_P, MID_R] = cin[q]

    per_q(enter)
    batch_start(0)
    static_start(1)
    lax.fori_loop(0, 8, send_guess, 0)
    static_wait(0)
    batch_wait(0)

    def edges(n):
        lane = lax.broadcasted_iota(jnp.int32, (n, PADR, LANES), 2)
        return lane == 0, lane == LANES - 1

    def up(a):
        return pltpu.roll(a, PADR - 1, 1)

    def down(a):
        return pltpu.roll(a, 1, 1)

    def right(a):
        return pltpu.roll(a, LANES - 1, 2)

    def left(a):
        return pltpu.roll(a, 1, 2)

    def forward(j, width, copy=None):
        def one(q):
            for lo, hi in chunks(width):
                n = hi - lo
                first, last = edges(n)
                uu = st[j, q, pl.ds(lo - 1, n + 2)]
                base = bb[pl.ds(lo - 1, n + 2)]
                kk = base * (1.0 + SLOPE * uu)
                u, k, b = uu[1:-1], kk[1:-1], base[1:-1]
                f = (kk[1:] + kk[:-1]) * (uu[1:] - uu[:-1])
                flow = f[1:] - f[:-1]
                f = (k + up(k)) * (up(u) - u)
                flow = flow + (f - down(f))
                f = (k + jnp.where(last, 0.0, right(k))) * (jnp.where(last, 0.0, right(u)) - u)
                flow = flow + (f - jnp.where(first, k * u, left(f)))
                new = jnp.where(b > 0.0, u + (0.5 * RATE) * flow, 0.0)
                st[j + 1, q, pl.ds(lo, n)] = new
                if copy is not None:
                    a, z_ = max(lo, H), min(hi, H + PLANES)
                    if a < z_:
                        st[copy, q, pl.ds(a, z_ - a)] = new[a - lo : z_ - lo]

        per_q(one)

    def coefficients(j, field=None):
        idx = j if field is None else field
        array, entry = PLACE[j]
        ref, off = coef[array], H - COEF_W[array]

        def one(q):
            for lo, hi in chunks(WIDTH[j]):
                n = hi - lo
                first, last = edges(n)
                uu = st[idx, q, pl.ds(lo - 1, n + 2)]
                base = bb[pl.ds(lo - 1, n + 2)]
                kk = (0.5 * RATE) * (base * (1.0 + SLOPE * uu))
                u, k = uu[1:-1], kk[1:-1]
                b = (0.25 * RATE) * base[1:-1]
                at = lambda i: (entry, q, i, pl.ds(lo - off, n))
                a, d = kk[1:] + kk[:-1], uu[1:] - uu[:-1]
                less, more = a[:-1] + b * d[:-1], a[1:] - b * d[1:]
                ref[at(1)] = less
                ref[at(2)] = more
                w_sum = less + more
                a, d = k + up(k), up(u) - u
                less, more = down(a) + b * down(d), a - b * d
                ref[at(3)] = less
                ref[at(4)] = more
                w_sum = w_sum + (less + more)
                a, d = k + right(k), right(u) - u
                less, more = left(a) + b * left(d), a - b * d
                ref[at(5)] = jnp.where(first, 0.0, less)
                ref[at(6)] = jnp.where(last, 0.0, more)
                edge = k + b * u
                w_sum = w_sum + (jnp.where(first, edge, less) + jnp.where(last, edge, more))
                ref[at(0)] = w_sum

        per_q(one)

    def change(vv, array, entry, q, lo, n):
        ref, off = coef[array], H - COEF_W[array]
        w = lambda i: ref[entry, q, i, pl.ds(lo - off, n)]
        v = vv[1:-1]
        acc = vv[:-2] * w(1) + vv[2:] * w(2)
        acc = acc + down(v) * w(3)
        acc = acc + up(v) * w(4)
        acc = acc + left(v) * w(5)
        acc = acc + right(v) * w(6)
        return acc - v * w(0)

    def field_of(j):
        return {2: U2, 6: U6}.get(j, j)

    def adjoint(idx, j, width):
        array, entry = PLACE[j]

        def one(q):
            for lo, hi in chunks(width):
                n = hi - lo
                vv = st[idx, q, pl.ds(lo - 1, n + 2)]
                new = (vv[1:-1] + change(vv, array, entry, q, lo, n)) + wt[pl.ds(lo, n)] * st[field_of(j), q, pl.ds(lo, n)]
                st[idx + 1, q, pl.ds(lo, n)] = jnp.where(bb[pl.ds(lo, n)] > 0.0, new, 0.0)

        per_q(one)

    def hop_copy():
        return pltpu.make_async_remote_copy(
            src_ref=g.at[0], dst_ref=gn, send_sem=hop_send, recv_sem=hop_recv,
            device_id=dev(px, (y + 3) % 4, z), device_id_type=MESH,
        )

    forward(0, 2)
    forward(1, 1, copy=U2)
    batch_start(U2)
    forward(2, 0)
    batch_start(3)
    static_wait(1)
    coefficients(0)
    coefficients(1)
    for i in range(8):
        arrived(g.at[i % 4, pl.ds(4 * (i // 4), 4)], gu_recv.at[i])

    @pl.when(y > 0)
    def _():
        hop_copy().start()

    batch_wait(3)
    forward(3, 3)
    forward(4, 2)
    forward(5, 1, copy=U6)
    batch_start(U6)
    forward(6, 0)
    batch_start(7)

    for q in range(3):
        st[RELAX, q, MID_P, MID_R] = g[q + 1]

    @pl.when(y < 3)
    def _():
        hop_copy().wait_recv()

    st[RELAX, 3, MID_P, MID_R] = gn[...]
    g0[pl.ds(0, PLANES), MID_R] = g[0]
    batch_start(RELAX)
    coefficients(3)
    batch_wait(U2)
    coefficients(2, U2)
    coefficients(5)
    coefficients(4)
    batch_wait(U6)
    coefficients(6, U6)
    batch_wait(7)
    coefficients(7)
    batch_wait(RELAX)

    for n in range(2):
        for i in range(4):
            adjoint(RELAX + 4 * n + i, 7 - 4 * n - i, 3 - i)
        batch_start(RELAX + 4 * n + 4)
        batch_wait(RELAX + 4 * n + 4)

    def err_field(i):
        return (
            lambda lo, m: err.at[i, pl.ds(lo, m)],
            lambda k, lo, m: eys.at[k, 0, pl.ds(lo, m)],
            lambda k, lo, m: eyh.at[k, 0, pl.ds(lo, m)],
        )

    cross = (err_field(4), err_field(0), lambda side: ce_send.at[side], lambda side: ce_recv.at[side])

    def block_copy():
        return pltpu.make_async_remote_copy(
            src_ref=eo, dst_ref=ei, send_sem=ce_send.at[8], recv_sem=ce_recv.at[8],
            device_id=dev(px, (y + 3) % 4, z), device_id_type=MESH,
        )

    def give(q, i, start):
        src = cor.at[q, pl.ds(4 * i, 4)]
        z_, px_ = 2 * (2 * c + i) + q // 2, x * 2 + q % 2
        if start:
            push(src, out.at[0, pl.ds(0, 4), pl.ds(pl.multiple_of(z * ROWS, ROWS), ROWS)], co_send.at[q, i], co_recv.at[z], px_, y, z_)
        else:
            push_done(src, co_send.at[q, i], px_, y, z_)

    @pl.when(y < 3)
    def _():
        halo_landed(cross[1], cross[3])
        block_copy().wait_recv()
        err[0, MID_P, MID_R] = ei[...]
        unpack(err.at[0], eyh.at[pl.ds(0, 2), 0])

    array, entry = PLACE[0]
    for i in range(4):
        q = 3 - i
        for lo, hi in chunks(3 - i):
            n = hi - lo
            vv = err[i, pl.ds(lo - 1, n + 2)]
            before = st[RELAX, q - 1, pl.ds(lo, n)] if q else g0[pl.ds(lo - H, n)]
            res = st[RELAX + 8, q, pl.ds(lo, n)] - before
            new = (vv[1:-1] + float(LEVELS) * change(vv, array, entry, q, lo, n)) + res
            err[i + 1, pl.ds(lo, n)] = jnp.where(bb[pl.ds(lo, n)] > 0.0, new, 0.0)

    @pl.when(y > 0)
    def _():
        eo[...] = err[4, MID_P, MID_R]
        pack(err.at[4], eys.at[pl.ds(0, 2), 0])
        block_copy().start()
        halo_start(*cross, y - 1)

    for q in range(4):
        st[FINAL, q, MID_P] = st[RELAX, q, MID_P] + err[3 - q, MID_P]
    batch_start(FINAL)
    for q in range(4):
        cor[q] = g[q] + err[4 - q, MID_P, MID_R]
        for k in range(2):
            give(q, k, True)

    total[...] = jnp.zeros(total.shape, F32)

    def spread(idx, j):
        def one(q):
            for lo, hi in chunks(0):
                n = hi - lo
                first, last = edges(n)
                uu = st[field_of(j), q, pl.ds(lo - 1, n + 2)]
                vv = st[idx, q, pl.ds(lo - 1, n + 2)]
                u, v = uu[1:-1], vv[1:-1]
                f = (uu[1:] - uu[:-1]) * (vv[1:] - vv[:-1])
                acc = f[1:] + f[:-1]
                f = (up(u) - u) * (up(v) - v)
                acc = acc + (f + down(f))
                f = (jnp.where(last, 0.0, right(u)) - u) * (jnp.where(last, 0.0, right(v)) - v)
                acc = acc + (f + jnp.where(first, u * v, left(f)))
                at = pl.ds(lo - H, n)
                total[at] = total[at] - ((0.5 * RATE) * (1.0 + SLOPE * u)) * acc

        per_q(one)

    batch_wait(FINAL)
    batch_sent(RELAX + 4)
    batch_sent(RELAX + 8)
    for i in range(4):
        adjoint(FINAL + i, 7 - i, 3 - i)
    batch_start(FINAL + 4)
    for i in range(4):
        spread(FINAL + i, 7 - i)
    batch_wait(FINAL + 4)
    for i in range(4, 8):
        if i < 7:
            adjoint(FINAL + i, 7 - i, 7 - i)
        spread(FINAL + i, 7 - i)

    turned[...] = jnp.transpose(total[:, pl.ds(H, ROWS)].reshape(PLANES * ROWS, LANES))

    def sum_copy(dy):
        y_ = (y + dy) % 4
        src = turned.at[pl.ds(pl.multiple_of(y_ * 32, 32), 32)]
        return pltpu.make_async_remote_copy(
            src_ref=src, dst_ref=sr.at[dy - 1], send_sem=r1_send.at[dy - 1], recv_sem=r1_recv.at[dy - 1],
            device_id=dev(px, y_, z), device_id_type=MESH,
        )

    for dy in range(1, 4):
        sum_copy(dy).start()
    part = turned[pl.ds(pl.multiple_of(y * 32, 32), 32)]
    for dy in range(1, 4):
        sum_copy(dy).wait_recv()
        part = part + sr[dy - 1]
    s2[0] = part
    s2[1] = pltpu.roll(part, 64, 1)

    def share(n, start):
        i, q = n // 4, n % 4
        src = s2.at[i, pl.ds(8 * q, 8)]
        z_, px_ = 2 * (2 * c + i) + q // 2, x * 2 + q % 2
        if start:
            push(src, sf.at[z], r2_send.at[n], r2_recv.at[z], px_, y, z_)
        else:
            push_done(src, r2_send.at[n], px_, y, z_)

    for n in range(8):
        share(n, True)
    for i in range(8):
        arrived(sf.at[i], r2_recv.at[i])
    sens_out[...] = sf[...]

    for n in range(8):
        share(n, False)
    for dy in range(1, 4):
        sum_copy(dy).wait_send()
    for q in range(4):
        for i in range(2):
            give(q, i, False)
    for i in range(8):
        arrived(out.at[0, pl.ds(0, 4), pl.ds(i * ROWS, ROWS)], co_recv.at[i])

    @pl.when(y > 0)
    def _():
        hop_copy().wait_send()
        block_copy().wait_send()
        halo_sent(*cross, y - 1)

    for idx in EXCHANGED:
        if idx not in (RELAX + 4, RELAX + 8):
            batch_sent(idx)
    for n in range(2):
        field, ssem, rsem = static_field(n)
        halo_sent(field, field, ssem, rsem, y, range(2, 8))

    for i in range(2):
        z_ = 2 * mine + i
        push_done(cut(base_src, z_), bs_send.at[i], to_px, y, z_)
        push_done(cut(weight, z_), wt_send.at[i], to_px, y, z_)

    def drain(i, carry):
        z_ = (z + i) % 8
        push_done(cut(ck.at[0], z_), ck_send.at[i], to_px, y, z_)
        push_done(cut(guess.at[0], z_), gu_send.at[i], to_px, y, z_)
        return carry

    lax.fori_loop(0, 8, drain, 0)


def on_device(checkpoints, guess, materials, table, weight):
    dma = pltpu.SemaphoreType.DMA
    vmem = lambda *shape: pltpu.VMEM(shape, F32)
    block = (PLANES, ROWS, LANES)
    corrected, shares = pl.pallas_call(
        kernel,
        out_shape=(
            jax.ShapeDtypeStruct(guess.shape, F32),
            jax.ShapeDtypeStruct((8, 8, LANES), F32),
        ),
        in_specs=[
            pl.BlockSpec(memory_space=pl.ANY),
            pl.BlockSpec(memory_space=pl.ANY),
            pl.BlockSpec(memory_space=pltpu.VMEM),
            pl.BlockSpec(memory_space=pltpu.SMEM),
            pl.BlockSpec(memory_space=pl.ANY),
        ],
        out_specs=(
            pl.BlockSpec(memory_space=pl.ANY),
            pl.BlockSpec(memory_space=pltpu.VMEM),
        ),
        scratch_shapes=[
            vmem(19, Q, PADP, PADR, LANES),
            vmem(len(EXCHANGED), 2, Q, 64, LANES),
            vmem(len(EXCHANGED), 2, Q, 32, LANES),
            vmem(2, Q, 7, 14, PADR, LANES),
            vmem(2, Q, 7, 12, PADR, LANES),
            vmem(2, Q, 7, 10, PADR, LANES),
            vmem(2, Q, 7, 14, PADR, LANES),
            vmem(4, 128, LANES),
            vmem(Q, *block),
            vmem(*block),
            vmem(*block),
            vmem(PADP, PADR, LANES),
            vmem(PADP, PADR, LANES),
            vmem(2, 2, 1, 64, LANES),
            vmem(2, 2, 1, 32, LANES),
            vmem(Q, *block),
            vmem(*block),
            vmem(PLANES, PADR, LANES),
            vmem(Q, *block),
            vmem(5, PADP, PADR, LANES),
            vmem(*block),
            vmem(*block),
            vmem(2, 1, 64, LANES),
            vmem(2, 1, 32, LANES),
            vmem(PLANES, PADR, LANES),
            vmem(LANES, LANES),
            vmem(3, 32, LANES),
            vmem(2, 32, LANES),
            vmem(8, 8, LANES),
            dma((8,)), dma((8,)), dma((8,)), dma((8,)),
            dma((2,)), dma((2,)), dma((2,)), dma((2,)),
            dma((2, 8)), dma((2, 8)),
            dma((len(EXCHANGED), 8)), dma((len(EXCHANGED), 8)),
            dma, dma,
            dma((9,)), dma((9,)),
            dma((4, 2)), dma((8,)),
            dma((3,)), dma((3,)), dma((8,)), dma((8,)),
        ],
        compiler_params=pltpu.CompilerParams(
            collective_id=0, has_side_effects=True, vmem_limit_bytes=60 * 1024 * 1024
        ),
    )(checkpoints, guess, materials, table, weight)
    parts = shares[:, :, :64].reshape(8, 8, 4, 16)
    sensitivity = jnp.transpose(parts, (2, 0, 3, 1)).reshape(4, 128, 8)
    return corrected, sensitivity


def solution(mesh):
    in_specs = (
        P("tm", "space", None, None),
        P("tm", "space", None, None),
        P("space", None, None),
        P(),
        P("space", None, None),
    )
    out_specs = (P("tm", "space", None, None), P("space", None, "tm"))
    return jax.shard_map(
        on_device, mesh=mesh, in_specs=in_specs, out_specs=out_specs, check_vma=False
    )
```

time: 179 us -> 122 us (0.68)
  Pallas kernels: 175 us -> 117 us
    pallas_call x1, Pallas kernels: 175 us -> 117 us  [on_device(): pl.pallas_call(kernel, out_shape=(jax.ShapeDtypeStruct(guess.shape, F32),...]
where the time goes in v2:
time: 122 us; the launch traced here: 120 us
  Pallas kernels  117 us (96%)
  local copies, waits for them, and re-layouts  2.41 us (2%)
    pallas_call x1, Pallas kernels, on_device(): pl.pallas_call(kernel, out_shape=(jax.ShapeDtypeStruct(guess.shape, F32),...  117 us

profile of v2, /device:TPU:17, one launch (start us, length us, event | category | flops | bytes accessed | tf_op | source)
XLA Modules:
  0.0 120.2 jit_solution(5376305919023802576)
XLA Ops:
  0.6 117.2 %shard_map.68 = (f32[1,4,128,128]{3,2,1,0:T(8,128)}, f32[8,8,128]{2,1,0:T(8,128)}) custom-call(f32[1,4,128,128]{3,2,1,0:T(8,128)} %ck.1, f32[1,4,128,128]{3,2,1,0:T(8,128)} %guess.1, s32[4,128,128]{2,1,0:T(8,128)} %mats.1, f32[8]{0:T(128)} %table.1, f32[4,128,128]{2,1,0:T(8,128)} %weight.1), custom_call_target="tpu_custom_call" | custom-call | tf_op jit(solution)/shard_map/pallas_call | solution.py:670
  117.8 0.0 copy-start
  117.8 0.9 reshape.10
  118.7 0.1 copy.7
  118.8 0.7 reshape.11
  119.5 0.0 copy-done
  119.5 0.7 copy.9
Async XLA Ops:
  117.8 1.7 %copy-start = (f32[1,4,128,128]{3,2,1,0:T(8,128)S(1)}, f32[1,4,128,128]{3,2,1,0:T(8,128)}, u32[]{:S(2)}) copy-start(f32[1,4,128,128]{3,2,1,0:T(8,128)} %get-tuple-element.8) | copy-start | bytes 786436

commit v3 on v2

v3 whole, which is shorter than its diff:
```python
import functools

import jax
import jax.numpy as jnp
from jax import lax
from jax.experimental import pallas as pl
from jax.experimental.pallas import tpu as pltpu
from jax.sharding import PartitionSpec as P

MESH = pl.DeviceIdType.MESH
F32 = jnp.float32

RATE = 0.006
SLOPE = 0.5
LEVELS = 8
Q, PLANES, ROWS, LANES, H = 4, 8, 16, 128, 4
PADP, PADR = PLANES + 2 * H, ROWS + 2 * H
MID_P, MID_R = pl.ds(H, PLANES), pl.ds(0, ROWS)
SIDES = [(-1, 0), (1, 0), (0, -1), (0, 1), (-1, -1), (1, -1), (-1, 1), (1, 1)]
OPPOSITE = [SIDES.index((-dx, -dz)) for dx, dz in SIDES]
RELAX, FINAL, U2, U6 = 8, 9, 17, 18
EXCHANGED = [0, 3, 7, U2, U6, RELAX, RELAX + 4, RELAX + 8, FINAL, FINAL + 4]
WIDTH = [3, 1, 2, 3, 0, 1, 2, 3]
PLACE = [(3, 1), (2, 1), (1, 1), (0, 1), (3, 0), (2, 0), (1, 0), (0, 0)]
COEF_W = [3, 2, 1, 3]
CORNER = [(1, 3, 0), (2, 2, 3), (3, 1, 5)]


def rows_of(width):
    return PADR if width else ROWS


def chunks(width):
    lo, hi = H - width, H + PLANES + width
    parts = -(-(hi - lo) // 5)
    edges = [lo + (hi - lo) * n // parts for n in range(parts + 1)]
    return list(zip(edges[:-1], edges[1:]))


def kernel(
    ck, guess, mats, table, weight,
    out, sens_out,
    st, yh, ys, zh_, zs_, c0, c1, c2, c3, base_src, bb, wt, bwh, bws, bzh, bzs, g, cor, err, eyh, eys, ezh, ezs,
    total, turned, sr, s2, sf,
    ck_send, ck_recv, gu_send, gu_recv, bs_send, bs_recv, wt_send, wt_recv,
    bx_send, bx_recv, ex_send, ex_recv, hop_send, hop_recv,
    ce_send, ce_recv, co_send, co_recv, r1_send, r1_recv, r2_send, r2_recv,
):
    coef = [c0, c1, c2, c3]
    t, s = lax.axis_index("tm"), lax.axis_index("space")
    y, zl, c = t // 4, (t // 2) % 2, t % 2
    x, zh = s // 4, s % 4
    z = zh * 2 + zl
    px = x * 2 + c
    mine = zl * 2 + c
    half = zh % 2

    def dev(px_, y_, z_):
        return {"tm": y_ * 4 + (z_ % 2) * 2 + px_ % 2, "space": (px_ // 2) * 4 + z_ // 2}

    def there(dx, dz):
        ok = jnp.bool_(True)
        if dx:
            ok = px > 0 if dx < 0 else px < 7
        if dz:
            ok_z = z > 0 if dz < 0 else z < 7
            ok = jnp.logical_and(ok, ok_z) if dx else ok_z
        return ok

    near = [(there(dx, dz), px + dx, z + dz) for dx, dz in SIDES]

    barrier = pltpu.get_barrier_semaphore()

    def greet(px_, y_, z_):
        pl.semaphore_signal(barrier, inc=1, device_id=dev(px_, y_, z_), device_id_type=MESH)

    def ring(i, carry):
        z_, px_ = i // 2, x * 2 + i % 2

        @pl.when(jnp.logical_or(z_ != z, px_ != px))
        def _():
            greet(px_, y, z_)

        return carry

    lax.fori_loop(0, 16, ring, 0)
    count = jnp.int32(15)
    far_ok = jnp.where(c == 0, px > 0, px < 7)
    far = jnp.where(c == 0, px - 1, px + 1)
    for dz in (-1, 0, 1):
        ok = jnp.logical_and(far_ok, there(0, dz)) if dz else far_ok

        @pl.when(ok)
        def _(dz=dz):
            greet(far, y, z + dz)

        count = count + ok.astype(jnp.int32)

    for dy in range(1, 4):
        greet(px, (y + dy) % 4, z)
    count = count + 3

    @pl.when(y > 0)
    def _():
        for z_ in range(8):
            greet(x * 2 + zh // 2, 0, z_)

    count = count + jnp.where(y == 0, 24, 0)
    for dy in (-1, 1):
        y_ok = jnp.logical_and(y + dy >= 0, y + dy < 4)
        for ok, px_, z_ in near:
            both = jnp.logical_and(ok, y_ok)

            @pl.when(both)
            def _(px_=px_, z_=z_, dy=dy):
                greet(px_, y + dy, z_)

            count = count + both.astype(jnp.int32)

    def lookup(p, carry):
        ids = mats[p]
        val = jnp.zeros(ids.shape, F32)
        for number in range(8):
            val = val + jnp.where(ids == number, table[number], 0.0)
        base_src[p] = val
        return carry

    lax.fori_loop(0, 4, lookup, 0)

    def clear_corners(axis, sign):
        for n in range(4):
            if SIDES[4 + n][axis] == sign:
                tile = jnp.zeros((8, LANES), F32)
                bzh[0, n, 0] = tile
                bzh[1, n, 0] = tile
                ezh[n, 0] = tile

                def clear(q, carry):
                    for e in range(len(EXCHANGED)):
                        zh_[e, n, q] = tile
                    return carry

                lax.fori_loop(0, Q, clear, 0)

    for side, lo in ((0, 0), (1, H + PLANES)):

        @pl.when(jnp.logical_not(near[side][0]))
        def _(side=side, lo=lo):
            slab = jnp.zeros((H, PADR, LANES), F32)
            for ref in (bb, wt, err.at[0]):
                ref[pl.ds(lo, H)] = slab

            def clear(q, carry):
                for idx in EXCHANGED:
                    st[idx, q, pl.ds(lo, H)] = slab
                return carry

            lax.fori_loop(0, Q, clear, 0)
            clear_corners(0, SIDES[side][0])

    for side, k in ((2, 0), (3, 1)):

        @pl.when(jnp.logical_not(near[side][0]))
        def _(side=side, k=k):
            edge = jnp.zeros((32, LANES), F32)
            for n in range(2):
                bwh[n, k, 0] = edge
            eyh[k, 0] = edge

            def clear(q, carry):
                for n in range(len(EXCHANGED)):
                    yh[n, k, q] = edge
                return carry

            lax.fori_loop(0, Q, clear, 0)
            clear_corners(1, SIDES[side][1])

    @pl.when(y == 3)
    def _():
        err[0] = jnp.zeros((PADP, PADR, LANES), F32)
        st[RELAX, 3, MID_P, MID_R] = jnp.zeros((PLANES, ROWS, LANES), F32)

    pl.semaphore_wait(barrier, count)

    def push(src, dst, ssem, rsem, px_, y_, z_):
        here = jnp.logical_and(jnp.logical_and(px_ == px, z_ == z), y_ == y)

        @pl.when(here)
        def _():
            pltpu.make_async_copy(src, dst, rsem).start()

        @pl.when(jnp.logical_not(here))
        def _():
            pltpu.make_async_remote_copy(
                src_ref=src, dst_ref=dst, send_sem=ssem, recv_sem=rsem,
                device_id=dev(px_, y_, z_), device_id_type=MESH,
            ).start()

    def push_done(src, ssem, px_, y_, z_):
        here = jnp.logical_and(jnp.logical_and(px_ == px, z_ == z), y_ == y)

        @pl.when(jnp.logical_not(here))
        def _():
            pltpu.make_async_copy(src, src, ssem).wait()

    def arrived(dst, rsem):
        pltpu.make_async_copy(dst, dst, rsem).wait()

    to_px = x * 2 + zh // 2
    slot = half * 4 + mine

    def cut(ref, z_):
        return ref.at[pl.ds(0, 4), pl.ds(pl.multiple_of(z_ * ROWS, ROWS), ROWS)]

    def send_ck(i, carry):
        z_ = (z + i) % 8
        push(cut(ck.at[0], z_), st.at[0, mine, pl.ds(H + 4 * half, 4), MID_R], ck_send.at[i], ck_recv.at[slot], to_px, y, z_)
        return carry

    def send_guess(i, carry):
        z_ = (z + i) % 8
        push(cut(guess.at[0], z_), g.at[mine, pl.ds(4 * half, 4)], gu_send.at[i], gu_recv.at[slot], to_px, y, z_)
        return carry

    for i in range(2):
        z_ = 2 * mine + i
        push(cut(base_src, z_), bb.at[pl.ds(H + 4 * half, 4), MID_R], bs_send.at[i], bs_recv.at[half], to_px, y, z_)
    lax.fori_loop(0, 8, send_ck, 0)
    for i in range(2):
        z_ = 2 * mine + i
        push(cut(weight, z_), wt.at[pl.ds(H + 4 * half, 4), MID_R], wt_send.at[i], wt_recv.at[half], to_px, y, z_)

    def outgoing(field, side):
        planes, rows_out, corner_out, _, _ = field
        dx, dz = SIDES[side]
        if dz == 0:
            return planes(H if dx < 0 else PLANES, H)
        return corner_out(side - 4) if dx else rows_out(0 if dz < 0 else 1)

    def landing(field, side):
        planes, _, _, rows_in, corner_in = field
        dx, dz = SIDES[side]
        if dz == 0:
            return planes(0 if dx < 0 else H + PLANES, H)
        return corner_in(side - 4) if dx else rows_in(0 if dz < 0 else 1)

    def halo_copy(field, to, side, ssem, rsem, y_):
        _, px_, z_ = near[side]
        back = OPPOSITE[side]
        return pltpu.make_async_remote_copy(
            src_ref=outgoing(field, side), dst_ref=landing(to, back), send_sem=ssem(side), recv_sem=rsem(back),
            device_id=dev(px_, y_, z_), device_id_type=MESH,
        )

    def halo_start(field, to, ssem, rsem, y_):
        for side in (4, 5, 6, 7, 2, 3, 0, 1):

            @pl.when(near[side][0])
            def _(side=side):
                halo_copy(field, to, side, ssem, rsem, y_).start()

    def halo_sent(field, to, ssem, rsem, y_, sides=range(8)):
        for side in sides:

            @pl.when(near[side][0])
            def _(side=side):
                halo_copy(field, to, side, ssem, rsem, y_).wait_send()

    def halo_landed(field, rsem):
        for side in range(8):

            @pl.when(near[side][0])
            def _(side=side):
                arrived(landing(field, side), rsem(side))

    def pack(block, rows_out, corner_out):
        for p in range(PLANES):
            for k, row in ((0, 0), (1, ROWS - H)):
                rows_out[0][rows_out[1](k, pl.ds(4 * p, 4))] = block[0][block[1](H + p, pl.ds(row, 4))]
        for n in range(4):
            dx, dz = SIDES[4 + n]
            for d, m, at in CORNER:
                plane = H + d - 1 if dx < 0 else H + PLANES - d
                row = 0 if dz < 0 else ROWS - m
                corner_out[0][corner_out[1](n, pl.ds(at, m))] = block[0][block[1](plane, pl.ds(row, m))]

    def unpack(block, rows_in, corner_in):
        for p in range(PLANES):
            for k, row in ((0, PADR - H), (1, ROWS)):
                block[0][block[1](H + p, pl.ds(row, 4))] = rows_in[0][rows_in[1](k, pl.ds(4 * p, 4))]
        for n in range(4):
            dx, dz = SIDES[4 + n]
            for d, m, at in CORNER:
                plane = H - d if dx < 0 else H + PLANES - 1 + d
                row = PADR - m if dz < 0 else ROWS
                block[0][block[1](plane, pl.ds(row, m))] = corner_in[0][corner_in[1](n, pl.ds(at, m))]

    def batch(idx):
        n = EXCHANGED.index(idx)
        all_q = pl.ds(0, Q)
        field = (
            lambda lo, m: st.at[idx, all_q, pl.ds(lo, m), MID_R],
            lambda k: ys.at[n, k],
            lambda k: zs_.at[n, k],
            lambda k: yh.at[n, k],
            lambda k: zh_.at[n, k],
        )
        return n, field, lambda side: ex_send.at[n, side], lambda side: ex_recv.at[n, side]

    def per_q(one):
        def body(q, carry):
            one(q)
            return carry

        lax.fori_loop(0, Q, body, 0)

    def batch_start(idx):
        n, field, ssem, rsem = batch(idx)
        at = lambda q: (lambda k, rows: (n, k, q, rows))
        per_q(lambda q: pack((st, lambda p, rows: (idx, q, p, rows)), (ys, at(q)), (zs_, at(q))))
        halo_start(field, field, ssem, rsem, y)

    def batch_wait(idx):
        n, field, ssem, rsem = batch(idx)
        halo_landed(field, rsem)
        at = lambda q: (lambda k, rows: (n, k, q, rows))
        per_q(lambda q: unpack((st, lambda p, rows: (idx, q, p, rows)), (yh, at(q)), (zh_, at(q))))

    def batch_sent(idx):
        n, field, ssem, rsem = batch(idx)
        halo_sent(field, field, ssem, rsem, y)

    def static_field(n):
        ref = bb if n == 0 else wt
        field = (
            lambda lo, m: ref.at[pl.ds(lo, m), MID_R],
            lambda k: bws.at[n, k, 0],
            lambda k: bzs.at[n, k, 0],
            lambda k: bwh.at[n, k, 0],
            lambda k: bzh.at[n, k, 0],
        )
        return field, lambda side: bx_send.at[n, side], lambda side: bx_recv.at[n, side]

    def static_start(n):
        ref, sem = (bb, bs_recv) if n == 0 else (wt, wt_recv)
        for i in range(2):
            arrived(ref.at[pl.ds(H + 4 * i, 4), MID_R], sem.at[i])
        at = lambda k, rows: (n, k, 0, rows)
        pack((ref, lambda p, rows: (p, rows)), (bws, at), (bzs, at))
        field, ssem, rsem = static_field(n)
        halo_start(field, field, ssem, rsem, y)

    def static_wait(n):
        field, ssem, rsem = static_field(n)
        halo_landed(field, rsem)
        at = lambda k, rows: (n, k, 0, rows)
        unpack((bb if n == 0 else wt, lambda p, rows: (p, rows)), (bwh, at), (bzh, at))

    static_start(0)
    for i in range(8):
        arrived(st.at[0, i % 4, pl.ds(H + 4 * (i // 4), 4), MID_R], ck_recv.at[i])
    batch_start(0)
    static_start(1)
    static_wait(0)
    batch_wait(0)
    lax.fori_loop(0, 4, send_guess, 0)

    def edges(n, rows):
        lane = lax.broadcasted_iota(jnp.int32, (n, rows, LANES), 2)
        return lane == 0, lane == LANES - 1

    def up(a):
        return pltpu.roll(a, PADR - 1, 1)

    def down(a):
        return pltpu.roll(a, 1, 1)

    def right(a):
        return pltpu.roll(a, LANES - 1, 2)

    def left(a):
        return pltpu.roll(a, 1, 2)

    def forward(j, width, copy=None):
        rows = rows_of(width)

        def one(q):
            for lo, hi in chunks(width):
                n = hi - lo
                first, last = edges(n, rows)
                uu = st[j, q, pl.ds(lo - 1, n + 2)]
                kk = bb[pl.ds(lo - 1, n + 2)] * (1.0 + SLOPE * uu)
                u, k = uu[1:-1], kk[1:-1]
                f = (k + up(k)) * (up(u) - u)
                flow = (f - down(f))[:, :rows]
                uu, kk, u, k = uu[:, :rows], kk[:, :rows], u[:, :rows], k[:, :rows]
                f = (kk[1:] + kk[:-1]) * (uu[1:] - uu[:-1])
                flow = flow + (f[1:] - f[:-1])
                f = (k + jnp.where(last, 0.0, right(k))) * (jnp.where(last, 0.0, right(u)) - u)
                flow = flow + (f - jnp.where(first, k * u, left(f)))
                new = u + (0.5 * RATE) * flow
                if width:
                    new = jnp.where(bb[pl.ds(lo, n)] > 0.0, new, 0.0)
                st[j + 1, q, pl.ds(lo, n), pl.ds(0, rows)] = new
                if copy is not None:
                    a, z_ = max(lo, H), min(hi, H + PLANES)
                    if a < z_:
                        st[copy, q, pl.ds(a, z_ - a), MID_R] = new[a - lo : z_ - lo, :ROWS]

        per_q(one)

    def coefficients(j, field=None):
        idx = j if field is None else field
        array, entry = PLACE[j]
        ref, off = coef[array], H - COEF_W[array]
        rows = rows_of(WIDTH[j])

        def one(q):
            for lo, hi in chunks(WIDTH[j]):
                n = hi - lo
                first, last = edges(n, rows)
                uu = st[idx, q, pl.ds(lo - 1, n + 2)]
                base = bb[pl.ds(lo - 1, n + 2)]
                kk = (0.5 * RATE) * (base * (1.0 + SLOPE * uu))
                u, k = uu[1:-1], kk[1:-1]
                b = (0.25 * RATE) * base[1:-1, :rows]
                at = lambda i: (entry, q, i, pl.ds(lo - off, n), pl.ds(0, rows))
                a, d = k + up(k), up(u) - u
                less, more = down(a)[:, :rows] + b * down(d)[:, :rows], a[:, :rows] - b * d[:, :rows]
                ref[at(3)] = less
                ref[at(4)] = more
                w_sum = less + more
                uu, kk, u, k = uu[:, :rows], kk[:, :rows], u[:, :rows], k[:, :rows]
                a, d = kk[1:] + kk[:-1], uu[1:] - uu[:-1]
                less, more = a[:-1] + b * d[:-1], a[1:] - b * d[1:]
                ref[at(1)] = less
                ref[at(2)] = more
                w_sum = w_sum + (less + more)
                a, d = k + right(k), right(u) - u
                less, more = left(a) + b * left(d), a - b * d
                ref[at(5)] = jnp.where(first, 0.0, less)
                ref[at(6)] = jnp.where(last, 0.0, more)
                edge = k + b * u
                w_sum = w_sum + (jnp.where(first, edge, less) + jnp.where(last, edge, more))
                ref[at(0)] = w_sum

        per_q(one)

    def change(vv, array, entry, q, lo, n, rows):
        ref, off = coef[array], H - COEF_W[array]
        w = lambda i: ref[entry, q, i, pl.ds(lo - off, n), pl.ds(0, rows)]
        acc = down(vv[1:-1])[:, :rows] * w(3)
        acc = acc + up(vv[1:-1])[:, :rows] * w(4)
        vv = vv[:, :rows]
        v = vv[1:-1]
        acc = acc + (vv[:-2] * w(1) + vv[2:] * w(2))
        acc = acc + left(v) * w(5)
        acc = acc + right(v) * w(6)
        return v, acc - v * w(0)

    def field_of(j):
        return {2: U2, 6: U6}.get(j, j)

    def adjoint(idx, j, width):
        array, entry = PLACE[j]
        rows = rows_of(width)
        some = pl.ds(0, rows)

        def one(q):
            for lo, hi in chunks(width):
                n = hi - lo
                at = pl.ds(lo, n)
                v, more = change(st[idx, q, pl.ds(lo - 1, n + 2)], array, entry, q, lo, n, rows)
                new = (v + more) + wt[at, some] * st[field_of(j), q, at, some]
                if width:
                    new = jnp.where(bb[at] > 0.0, new, 0.0)
                st[idx + 1, q, at, some] = new

        per_q(one)

    def hop_copy():
        return pltpu.make_async_remote_copy(
            src_ref=g.at[0], dst_ref=st.at[RELAX, 3, MID_P, MID_R], send_sem=hop_send, recv_sem=hop_recv,
            device_id=dev(px, (y + 3) % 4, z), device_id_type=MESH,
        )

    forward(0, 2)
    forward(1, 1, copy=U2)
    forward(2, 0)
    batch_start(3)

    def rest(i, carry):
        return send_guess(i + 4, carry)

    lax.fori_loop(0, 4, rest, 0)
    static_wait(1)
    coefficients(0)
    coefficients(1)
    batch_wait(3)
    batch_start(U2)
    forward(3, 3)
    for i in range(8):
        arrived(g.at[i % 4, pl.ds(4 * (i // 4), 4)], gu_recv.at[i])

    @pl.when(y > 0)
    def _():
        hop_copy().start()

    for q in range(3):
        st[RELAX, q, MID_P, MID_R] = g[q + 1]
    forward(4, 2)
    forward(5, 1, copy=U6)
    forward(6, 0)
    batch_start(7)

    @pl.when(y < 3)
    def _():
        hop_copy().wait_recv()

    batch_start(RELAX)
    batch_start(U6)
    coefficients(3)
    coefficients(5)
    coefficients(4)
    batch_wait(U2)
    coefficients(2, U2)
    batch_wait(7)
    coefficients(7)
    batch_wait(U6)
    coefficients(6, U6)
    batch_wait(RELAX)

    for n in range(2):
        for i in range(4):
            adjoint(RELAX + 4 * n + i, 7 - 4 * n - i, 3 - i)
        batch_start(RELAX + 4 * n + 4)
        batch_wait(RELAX + 4 * n + 4)

    def err_field(i):
        return (
            lambda lo, m: err.at[i, pl.ds(lo, m), MID_R],
            lambda k: eys.at[k, 0],
            lambda k: ezs.at[k, 0],
            lambda k: eyh.at[k, 0],
            lambda k: ezh.at[k, 0],
        )

    cross = (err_field(4), err_field(0), lambda side: ce_send.at[side], lambda side: ce_recv.at[side])

    def block_copy():
        return pltpu.make_async_remote_copy(
            src_ref=err.at[4, MID_P, MID_R], dst_ref=err.at[0, MID_P, MID_R], send_sem=ce_send.at[8], recv_sem=ce_recv.at[8],
            device_id=dev(px, (y + 3) % 4, z), device_id_type=MESH,
        )

    def packed(k, rows):
        return (k, 0, rows)

    def give(q, i, start):
        src = cor.at[q, pl.ds(4 * i, 4)]
        z_, px_ = 2 * (2 * c + i) + q // 2, x * 2 + q % 2
        if start:
            push(src, out.at[0, pl.ds(0, 4), pl.ds(pl.multiple_of(z * ROWS, ROWS), ROWS)], co_send.at[q, i], co_recv.at[z], px_, y, z_)
        else:
            push_done(src, co_send.at[q, i], px_, y, z_)

    @pl.when(y < 3)
    def _():
        halo_landed(cross[1], cross[3])
        block_copy().wait_recv()
        unpack((err, lambda p, rows: (0, p, rows)), (eyh, packed), (ezh, packed))

    array, entry = PLACE[0]
    for i in range(4):
        q = 3 - i
        rows = rows_of(3 - i)
        some = pl.ds(0, rows)
        for lo, hi in chunks(3 - i):
            n = hi - lo
            at = pl.ds(lo, n)
            e, more = change(err[i, pl.ds(lo - 1, n + 2)], array, entry, q, lo, n, rows)
            before = st[RELAX, q - 1, at, some] if q else g[0, pl.ds(lo - H, n)]
            res = st[RELAX + 8, q, at, some] - before
            new = (e + float(LEVELS) * more) + res
            if i < 3:
                new = jnp.where(bb[at] > 0.0, new, 0.0)
            err[i + 1, at, some] = new

    @pl.when(y > 0)
    def _():
        block_copy().start()
        pack((err, lambda p, rows: (4, p, rows)), (eys, packed), (ezs, packed))
        halo_start(*cross, y - 1)

    for q in range(4):
        st[FINAL, q, MID_P, MID_R] = st[RELAX, q, MID_P, MID_R] + err[3 - q, MID_P, MID_R]
    batch_start(FINAL)
    for q in range(4):
        cor[q] = g[q] + err[4 - q, MID_P, MID_R]

    total[...] = jnp.zeros(total.shape, F32)

    def spread(idx, j):
        def one(q):
            for lo, hi in chunks(0):
                n = hi - lo
                first, last = edges(n, ROWS)
                uu = st[field_of(j), q, pl.ds(lo - 1, n + 2)]
                vv = st[idx, q, pl.ds(lo - 1, n + 2)]
                u, v = uu[1:-1], vv[1:-1]
                f = (up(u) - u) * (up(v) - v)
                acc = (f + down(f))[:, :ROWS]
                uu, vv, u, v = uu[:, :ROWS], vv[:, :ROWS], u[:, :ROWS], v[:, :ROWS]
                f = (uu[1:] - uu[:-1]) * (vv[1:] - vv[:-1])
                acc = acc + (f[1:] + f[:-1])
                f = (jnp.where(last, 0.0, right(u)) - u) * (jnp.where(last, 0.0, right(v)) - v)
                acc = acc + (f + jnp.where(first, u * v, left(f)))
                at = pl.ds(lo - H, n)
                total[at] = total[at] - ((0.5 * RATE) * (1.0 + SLOPE * u)) * acc

        per_q(one)

    batch_wait(FINAL)
    batch_sent(RELAX + 4)
    batch_sent(RELAX + 8)
    for i in range(4):
        adjoint(FINAL + i, 7 - i, 3 - i)
    batch_start(FINAL + 4)
    for i in range(4):
        spread(FINAL + i, 7 - i)
    batch_wait(FINAL + 4)
    for q in range(4):
        for k in range(2):
            give(q, k, True)
    for i in range(4, 8):
        if i < 7:
            adjoint(FINAL + i, 7 - i, 7 - i)
        spread(FINAL + i, 7 - i)

    turned[...] = jnp.transpose(total[...].reshape(PLANES * ROWS, LANES))

    def sum_copy():
        return pltpu.make_async_remote_copy(
            src_ref=turned, dst_ref=sr.at[jnp.maximum(y - 1, 0)], send_sem=r1_send, recv_sem=r1_recv.at[jnp.maximum(y - 1, 0)],
            device_id=dev(px, 0, z), device_id_type=MESH,
        )

    def share(n, start):
        y_, i, q = n // 8, (n // 4) % 2, n % 4
        src = s2.at[i, pl.ds(pl.multiple_of(32 * y_ + 8 * q, 8), 8)]
        z_, px_ = 2 * (2 * c + i) + q // 2, x * 2 + q % 2
        if start:
            push(src, sf.at[z], r2_send.at[n], r2_recv.at[z], px_, y_, z_)
        else:
            push_done(src, r2_send.at[n], px_, y_, z_)

    def share_start(n, carry):
        share(n, True)
        return carry

    def share_done(n, carry):
        share(n, False)
        return carry

    @pl.when(y > 0)
    def _():
        sum_copy().start()

    @pl.when(y == 0)
    def _():
        part = turned[...]
        for n in range(3):
            arrived(sr.at[n], r1_recv.at[n])
            part = part + sr[n]
        s2[0] = part
        s2[1] = pltpu.roll(part, 64, 1)
        lax.fori_loop(0, 32, share_start, 0)

    for i in range(8):
        arrived(sf.at[i], r2_recv.at[i])
    sens_out[...] = sf[...]

    @pl.when(y > 0)
    def _():
        sum_copy().wait_send()

    @pl.when(y == 0)
    def _():
        lax.fori_loop(0, 32, share_done, 0)

    for q in range(4):
        for i in range(2):
            give(q, i, False)
    for i in range(8):
        arrived(out.at[0, pl.ds(0, 4), pl.ds(i * ROWS, ROWS)], co_recv.at[i])

    @pl.when(y > 0)
    def _():
        hop_copy().wait_send()
        block_copy().wait_send()
        halo_sent(*cross, y - 1)

    for idx in EXCHANGED:
        if idx not in (RELAX + 4, RELAX + 8):
            batch_sent(idx)
    for n in range(2):
        field, ssem, rsem = static_field(n)
        halo_sent(field, field, ssem, rsem, y)

    for i in range(2):
        z_ = 2 * mine + i
        push_done(cut(base_src, z_), bs_send.at[i], to_px, y, z_)
        push_done(cut(weight, z_), wt_send.at[i], to_px, y, z_)

    def drain(i, carry):
        z_ = (z + i) % 8
        push_done(cut(ck.at[0], z_), ck_send.at[i], to_px, y, z_)
        push_done(cut(guess.at[0], z_), gu_send.at[i], to_px, y, z_)
        return carry

    lax.fori_loop(0, 8, drain, 0)


def on_device(checkpoints, guess, materials, table, weight):
    dma = pltpu.SemaphoreType.DMA
    vmem = lambda *shape: pltpu.VMEM(shape, F32)
    block = (PLANES, ROWS, LANES)
    corrected, shares = pl.pallas_call(
        kernel,
        out_shape=(
            jax.ShapeDtypeStruct(guess.shape, F32),
            jax.ShapeDtypeStruct((8, 8, LANES), F32),
        ),
        in_specs=[
            pl.BlockSpec(memory_space=pl.ANY),
            pl.BlockSpec(memory_space=pl.ANY),
            pl.BlockSpec(memory_space=pltpu.VMEM),
            pl.BlockSpec(memory_space=pltpu.SMEM),
            pl.BlockSpec(memory_space=pl.ANY),
        ],
        out_specs=(
            pl.BlockSpec(memory_space=pl.ANY),
            pl.BlockSpec(memory_space=pltpu.VMEM),
        ),
        scratch_shapes=[
            vmem(19, Q, PADP, PADR, LANES),
            vmem(len(EXCHANGED), 2, Q, 32, LANES),
            vmem(len(EXCHANGED), 2, Q, 32, LANES),
            vmem(len(EXCHANGED), 4, Q, 8, LANES),
            vmem(len(EXCHANGED), 4, Q, 8, LANES),
            vmem(2, Q, 7, 14, PADR, LANES),
            vmem(2, Q, 7, 12, PADR, LANES),
            vmem(2, Q, 7, 10, PADR, LANES),
            vmem(2, Q, 7, 14, PADR, LANES),
            vmem(4, 128, LANES),
            vmem(PADP, PADR, LANES),
            vmem(PADP, PADR, LANES),
            vmem(2, 2, 1, 32, LANES),
            vmem(2, 2, 1, 32, LANES),
            vmem(2, 4, 1, 8, LANES),
            vmem(2, 4, 1, 8, LANES),
            vmem(Q, *block),
            vmem(Q, *block),
            vmem(5, PADP, PADR, LANES),
            vmem(2, 1, 32, LANES),
            vmem(2, 1, 32, LANES),
            vmem(4, 1, 8, LANES),
            vmem(4, 1, 8, LANES),
            vmem(*block),
            vmem(LANES, LANES),
            vmem(3, LANES, LANES),
            vmem(2, LANES, LANES),
            vmem(8, 8, LANES),
            dma((8,)), dma((8,)), dma((8,)), dma((8,)),
            dma((2,)), dma((2,)), dma((2,)), dma((2,)),
            dma((2, 8)), dma((2, 8)),
            dma((len(EXCHANGED), 8)), dma((len(EXCHANGED), 8)),
            dma, dma,
            dma((9,)), dma((9,)),
            dma((4, 2)), dma((8,)),
            dma, dma((3,)), dma((32,)), dma((8,)),
        ],
        compiler_params=pltpu.CompilerParams(
            collective_id=0, has_side_effects=True, vmem_limit_bytes=60 * 1024 * 1024
        ),
    )(checkpoints, guess, materials, table, weight)
    parts = shares[:, :, :64].reshape(8, 8, 4, 16)
    sensitivity = jnp.transpose(parts, (2, 0, 3, 1)).reshape(4, 128, 8)
    return corrected, sensitivity


def solution(mesh):
    in_specs = (
        P("tm", "space", None, None),
        P("tm", "space", None, None),
        P("space", None, None),
        P(),
        P("space", None, None),
    )
    out_specs = (P("tm", "space", None, None), P("space", None, "tm"))
    return jax.shard_map(
        on_device, mesh=mesh, in_specs=in_specs, out_specs=out_specs, check_vma=False
    )
```

time: 122 us -> 112 us (0.918)
  Pallas kernels: 117 us -> 108 us
    pallas_call x1, Pallas kernels: 117 us -> 108 us  [on_device(): pl.pallas_call(kernel, out_shape=(jax.ShapeDtypeStruct(guess.shape, F32),...]
where the time goes in v3:
time: 112 us; the launch traced here: 111 us
  Pallas kernels  108 us (96%)
  local copies, waits for them, and re-layouts  2.41 us (2%)
    pallas_call x1, Pallas kernels, on_device(): pl.pallas_call(kernel, out_shape=(jax.ShapeDtypeStruct(guess.shape, F32),...  108 us

profile of v3, /device:TPU:17, one launch (start us, length us, event | category | flops | bytes accessed | tf_op | source)
XLA Modules:
  0.0 111.0 jit_solution(4919192869118259171)
XLA Ops:
  0.6 108.0 %shard_map.68 = (f32[1,4,128,128]{3,2,1,0:T(8,128)}, f32[8,8,128]{2,1,0:T(8,128)}) custom-call(f32[1,4,128,128]{3,2,1,0:T(8,128)} %ck.1, f32[1,4,128,128]{3,2,1,0:T(8,128)} %guess.1, s32[4,128,128]{2,1,0:T(8,128)} %mats.1, f32[8]{0:T(128)} %table.1, f32[4,128,128]{2,1,0:T(8,128)} %weight.1), custom_call_target="tpu_custom_call" | custom-call | tf_op jit(solution)/shard_map/pallas_call | solution.py:728
  108.6 0.0 copy-start
  108.6 0.9 reshape.10
  109.5 0.1 copy.7
  109.6 0.7 reshape.11
  110.3 0.0 copy-done
  110.3 0.7 copy.9
Async XLA Ops:
  108.6 1.7 %copy-start = (f32[1,4,128,128]{3,2,1,0:T(8,128)S(1)}, f32[1,4,128,128]{3,2,1,0:T(8,128)}, u32[]{:S(2)}) copy-start(f32[1,4,128,128]{3,2,1,0:T(8,128)} %get-tuple-element.8) | copy-start | bytes 786436

commit v4 on v3

--- a/solution.py
+++ b/solution.py
@@ -20,6 +20,7 @@
 OPPOSITE = [SIDES.index((-dx, -dz)) for dx, dz in SIDES]
 RELAX, FINAL, U2, U6 = 8, 9, 17, 18
 EXCHANGED = [0, 3, 7, U2, U6, RELAX, RELAX + 4, RELAX + 8, FINAL, FINAL + 4]
+SOME = {RELAX + 8: (1, 3), FINAL: (0, 3)}
 WIDTH = [3, 1, 2, 3, 0, 1, 2, 3]
 PLACE = [(3, 1), (2, 1), (1, 1), (0, 1), (3, 0), (2, 0), (1, 0), (0, 0)]
 COEF_W = [3, 2, 1, 3]
@@ -41,7 +42,7 @@
     ck, guess, mats, table, weight,
     out, sens_out,
     st, yh, ys, zh_, zs_, c0, c1, c2, c3, base_src, bb, wt, bwh, bws, bzh, bzs, g, cor, err, eyh, eys, ezh, ezs,
-    total, turned, sr, s2, sf,
+    total, turned, sr, s2, sf, ids_, id_sem,
     ck_send, ck_recv, gu_send, gu_recv, bs_send, bs_recv, wt_send, wt_recv,
     bx_send, bx_recv, ex_send, ex_recv, hop_send, hop_recv,
     ce_send, ce_recv, co_send, co_recv, r1_send, r1_recv, r2_send, r2_recv,
@@ -70,6 +71,8 @@
     near = [(there(dx, dz), px + dx, z + dz) for dx, dz in SIDES]
 
     barrier = pltpu.get_barrier_semaphore()
+    fetch = pltpu.make_async_copy(mats, ids_, id_sem)
+    fetch.start()
 
     def greet(px_, y_, z_):
         pl.semaphore_signal(barrier, inc=1, device_id=dev(px_, y_, z_), device_id_type=MESH)
@@ -106,25 +109,23 @@
             greet(x * 2 + zh // 2, 0, z_)
 
     count = count + jnp.where(y == 0, 24, 0)
-    for dy in (-1, 1):
-        y_ok = jnp.logical_and(y + dy >= 0, y + dy < 4)
-        for ok, px_, z_ in near:
-            both = jnp.logical_and(ok, y_ok)
-
-            @pl.when(both)
-            def _(px_=px_, z_=z_, dy=dy):
-                greet(px_, y + dy, z_)
-
-            count = count + both.astype(jnp.int32)
+    for ok, px_, z_ in near:
+
+        @pl.when(jnp.logical_and(ok, y < 3))
+        def _(px_=px_, z_=z_):
+            greet(px_, y + 1, z_)
+
+        count = count + jnp.logical_and(ok, y > 0).astype(jnp.int32)
 
     def lookup(p, carry):
-        ids = mats[p]
+        ids = ids_[p]
         val = jnp.zeros(ids.shape, F32)
         for number in range(8):
             val = val + jnp.where(ids == number, table[number], 0.0)
         base_src[p] = val
         return carry
 
+    fetch.wait()
     lax.fori_loop(0, 4, lookup, 0)
 
     def clear_corners(axis, sign):
@@ -212,13 +213,17 @@
     def cut(ref, z_):
         return ref.at[pl.ds(0, 4), pl.ds(pl.multiple_of(z_ * ROWS, ROWS), ROWS)]
 
+    def turn(i):
+        k = (i + 1) // 2
+        return (z + jnp.where(i % 2 == 0, 4 + k, 4 - k)) % 8
+
     def send_ck(i, carry):
-        z_ = (z + i) % 8
+        z_ = turn(i)
         push(cut(ck.at[0], z_), st.at[0, mine, pl.ds(H + 4 * half, 4), MID_R], ck_send.at[i], ck_recv.at[slot], to_px, y, z_)
         return carry
 
     def send_guess(i, carry):
-        z_ = (z + i) % 8
+        z_ = turn(i)
         push(cut(guess.at[0], z_), g.at[mine, pl.ds(4 * half, 4)], gu_send.at[i], gu_recv.at[slot], to_px, y, z_)
         return carry
 
@@ -226,9 +231,6 @@
         z_ = 2 * mine + i
         push(cut(base_src, z_), bb.at[pl.ds(H + 4 * half, 4), MID_R], bs_send.at[i], bs_recv.at[half], to_px, y, z_)
     lax.fori_loop(0, 8, send_ck, 0)
-    for i in range(2):
-        z_ = 2 * mine + i
-        push(cut(weight, z_), wt.at[pl.ds(H + 4 * half, 4), MID_R], wt_send.at[i], wt_recv.at[half], to_px, y, z_)
 
     def outgoing(field, side):
         planes, rows_out, corner_out, _, _ = field
@@ -252,8 +254,8 @@
             device_id=dev(px_, y_, z_), device_id_type=MESH,
         )
 
-    def halo_start(field, to, ssem, rsem, y_):
-        for side in (4, 5, 6, 7, 2, 3, 0, 1):
+    def halo_start(field, to, ssem, rsem, y_, sides):
+        for side in sides:
 
             @pl.when(near[side][0])
             def _(side=side):
@@ -273,16 +275,18 @@
             def _(side=side):
                 arrived(landing(field, side), rsem(side))
 
-    def pack(block, rows_out, corner_out):
-        for p in range(PLANES):
-            for k, row in ((0, 0), (1, ROWS - H)):
-                rows_out[0][rows_out[1](k, pl.ds(4 * p, 4))] = block[0][block[1](H + p, pl.ds(row, 4))]
+    def pack_corners(block, corner_out):
         for n in range(4):
             dx, dz = SIDES[4 + n]
             for d, m, at in CORNER:
                 plane = H + d - 1 if dx < 0 else H + PLANES - d
                 row = 0 if dz < 0 else ROWS - m
                 corner_out[0][corner_out[1](n, pl.ds(at, m))] = block[0][block[1](plane, pl.ds(row, m))]
+
+    def pack_rows(block, rows_out):
+        for p in range(PLANES):
+            for k, row in ((0, 0), (1, ROWS - H)):
+                rows_out[0][rows_out[1](k, pl.ds(4 * p, 4))] = block[0][block[1](H + p, pl.ds(row, 4))]
 
     def unpack(block, rows_in, corner_in):
         for p in range(PLANES):
@@ -297,34 +301,38 @@
 
     def batch(idx):
         n = EXCHANGED.index(idx)
-        all_q = pl.ds(0, Q)
+        some = pl.ds(*SOME.get(idx, (0, Q)))
         field = (
-            lambda lo, m: st.at[idx, all_q, pl.ds(lo, m), MID_R],
-            lambda k: ys.at[n, k],
-            lambda k: zs_.at[n, k],
-            lambda k: yh.at[n, k],
-            lambda k: zh_.at[n, k],
+            lambda lo, m: st.at[idx, some, pl.ds(lo, m), MID_R],
+            lambda k: ys.at[n, k, some],
+            lambda k: zs_.at[n, k, some],
+            lambda k: yh.at[n, k, some],
+            lambda k: zh_.at[n, k, some],
         )
         return n, field, lambda side: ex_send.at[n, side], lambda side: ex_recv.at[n, side]
 
-    def per_q(one):
+    def per_q(one, idx=None):
         def body(q, carry):
             one(q)
             return carry
 
-        lax.fori_loop(0, Q, body, 0)
+        lo, m = SOME.get(idx, (0, Q))
+        lax.fori_loop(lo, lo + m, body, 0)
 
     def batch_start(idx):
         n, field, ssem, rsem = batch(idx)
         at = lambda q: (lambda k, rows: (n, k, q, rows))
-        per_q(lambda q: pack((st, lambda p, rows: (idx, q, p, rows)), (ys, at(q)), (zs_, at(q))))
-        halo_start(field, field, ssem, rsem, y)
+        block = lambda q: (st, lambda p, rows: (idx, q, p, rows))
+        per_q(lambda q: pack_corners(block(q), (zs_, at(q))), idx)
+        halo_start(field, field, ssem, rsem, y, (4, 5, 6, 7))
+        per_q(lambda q: pack_rows(block(q), (ys, at(q))), idx)
+        halo_start(field, field, ssem, rsem, y, (2, 3, 0, 1))
 
     def batch_wait(idx):
         n, field, ssem, rsem = batch(idx)
         halo_landed(field, rsem)
         at = lambda q: (lambda k, rows: (n, k, q, rows))
-        per_q(lambda q: unpack((st, lambda p, rows: (idx, q, p, rows)), (yh, at(q)), (zh_, at(q))))
+        per_q(lambda q: unpack((st, lambda p, rows: (idx, q, p, rows)), (yh, at(q)), (zh_, at(q))), idx)
 
     def batch_sent(idx):
         n, field, ssem, rsem = batch(idx)
@@ -346,9 +354,11 @@
         for i in range(2):
             arrived(ref.at[pl.ds(H + 4 * i, 4), MID_R], sem.at[i])
         at = lambda k, rows: (n, k, 0, rows)
-        pack((ref, lambda p, rows: (p, rows)), (bws, at), (bzs, at))
+        block = (ref, lambda p, rows: (p, rows))
+        pack_corners(block, (bzs, at))
+        pack_rows(block, (bws, at))
         field, ssem, rsem = static_field(n)
-        halo_start(field, field, ssem, rsem, y)
+        halo_start(field, field, ssem, rsem, y, (4, 5, 6, 7, 2, 3, 0, 1))
 
     def static_wait(n):
         field, ssem, rsem = static_field(n)
@@ -360,7 +370,9 @@
     for i in range(8):
         arrived(st.at[0, i % 4, pl.ds(H + 4 * (i // 4), 4), MID_R], ck_recv.at[i])
     batch_start(0)
-    static_start(1)
+    for i in range(2):
+        z_ = 2 * mine + i
+        push(cut(weight, z_), wt.at[pl.ds(H + 4 * half, 4), MID_R], wt_send.at[i], wt_recv.at[half], to_px, y, z_)
     static_wait(0)
     batch_wait(0)
     lax.fori_loop(0, 4, send_guess, 0)
@@ -488,14 +500,15 @@
     forward(1, 1, copy=U2)
     forward(2, 0)
     batch_start(3)
+    static_start(1)
 
     def rest(i, carry):
         return send_guess(i + 4, carry)
 
     lax.fori_loop(0, 4, rest, 0)
-    static_wait(1)
     coefficients(0)
     coefficients(1)
+    static_wait(1)
     batch_wait(3)
     batch_start(U2)
     forward(3, 3)
@@ -512,29 +525,31 @@
     forward(5, 1, copy=U6)
     forward(6, 0)
     batch_start(7)
+    batch_start(U6)
 
     @pl.when(y < 3)
     def _():
         hop_copy().wait_recv()
 
     batch_start(RELAX)
-    batch_start(U6)
-    coefficients(3)
     coefficients(5)
     coefficients(4)
-    batch_wait(U2)
-    coefficients(2, U2)
     batch_wait(7)
     coefficients(7)
     batch_wait(U6)
     coefficients(6, U6)
     batch_wait(RELAX)
-
-    for n in range(2):
-        for i in range(4):
-            adjoint(RELAX + 4 * n + i, 7 - 4 * n - i, 3 - i)
-        batch_start(RELAX + 4 * n + 4)
-        batch_wait(RELAX + 4 * n + 4)
+    for i in range(4):
+        adjoint(RELAX + i, 7 - i, 3 - i)
+    batch_start(RELAX + 4)
+    coefficients(3)
+    batch_wait(U2)
+    coefficients(2, U2)
+    batch_wait(RELAX + 4)
+    for i in range(4, 8):
+        adjoint(RELAX + i, 7 - i, 7 - i)
+    batch_start(RELAX + 8)
+    batch_wait(RELAX + 8)
 
     def err_field(i):
         return (
@@ -570,9 +585,9 @@
         block_copy().wait_recv()
         unpack((err, lambda p, rows: (0, p, rows)), (eyh, packed), (ezh, packed))
 
-    array, entry = PLACE[0]
-    for i in range(4):
+    def coarse(i):
         q = 3 - i
+        array, entry = PLACE[0]
         rows = rows_of(3 - i)
         some = pl.ds(0, rows)
         for lo, hi in chunks(3 - i):
@@ -586,15 +601,28 @@
                 new = jnp.where(bb[at] > 0.0, new, 0.0)
             err[i + 1, at, some] = new
 
+    for i in range(3):
+        coarse(i)
+
     @pl.when(y > 0)
     def _():
+        coarse(3)
+        block = (err, lambda p, rows: (4, p, rows))
+        pack_corners(block, (ezs, packed))
+        halo_start(*cross, y - 1, (4, 5, 6, 7))
+        pack_rows(block, (eys, packed))
+        halo_start(*cross, y - 1, (2, 3, 0, 1))
         block_copy().start()
-        pack((err, lambda p, rows: (4, p, rows)), (eys, packed), (ezs, packed))
-        halo_start(*cross, y - 1)
-
-    for q in range(4):
+
+    for q in range(3):
         st[FINAL, q, MID_P, MID_R] = st[RELAX, q, MID_P, MID_R] + err[3 - q, MID_P, MID_R]
     batch_start(FINAL)
+    st[FINAL, 3] = st[RELAX, 3] + err[0]
+
+    @pl.when(y == 0)
+    def _():
+        coarse(3)
+
     for q in range(4):
         cor[q] = g[q] + err[4 - q, MID_P, MID_R]
 
@@ -713,7 +741,7 @@
         push_done(cut(weight, z_), wt_send.at[i], to_px, y, z_)
 
     def drain(i, carry):
-        z_ = (z + i) % 8
+        z_ = turn(i)
         push_done(cut(ck.at[0], z_), ck_send.at[i], to_px, y, z_)
         push_done(cut(guess.at[0], z_), gu_send.at[i], to_px, y, z_)
         return carry
@@ -734,7 +762,7 @@
         in_specs=[
             pl.BlockSpec(memory_space=pl.ANY),
             pl.BlockSpec(memory_space=pl.ANY),
-            pl.BlockSpec(memory_space=pltpu.VMEM),
+            pl.BlockSpec(memory_space=pl.ANY),
             pl.BlockSpec(memory_space=pltpu.SMEM),
             pl.BlockSpec(memory_space=pl.ANY),
         ],
@@ -771,6 +799,8 @@
             vmem(3, LANES, LANES),
             vmem(2, LANES, LANES),
             vmem(8, 8, LANES),
+            pltpu.VMEM((4, 128, LANES), jnp.int32),
+            dma,
             dma((8,)), dma((8,)), dma((8,)), dma((8,)),
             dma((2,)), dma((2,)), dma((2,)), dma((2,)),
             dma((2, 8)), dma((2, 8)),

time: 112 us -> 109 us (0.973)
  Pallas kernels: 108 us -> 105 us
    pallas_call x1, Pallas kernels: 108 us -> 105 us  [on_device(): pl.pallas_call(kernel, out_shape=(jax.ShapeDtypeStruct(guess.shape, F32),...]
where the time goes in v4:
time: 109 us; the launch traced here: 108 us
  Pallas kernels  105 us (96%)
  local copies, waits for them, and re-layouts  2.41 us (2%)
    pallas_call x1, Pallas kernels, on_device(): pl.pallas_call(kernel, out_shape=(jax.ShapeDtypeStruct(guess.shape, F32),...  105 us

profile of v4, /device:TPU:17, one launch (start us, length us, event | category | flops | bytes accessed | tf_op | source)
XLA Modules:
  0.0 107.7 jit_solution(4759851690048862586)
XLA Ops:
  0.6 104.6 %shard_map.68 = (f32[1,4,128,128]{3,2,1,0:T(8,128)}, f32[8,8,128]{2,1,0:T(8,128)}) custom-call(f32[1,4,128,128]{3,2,1,0:T(8,128)} %ck.1, f32[1,4,128,128]{3,2,1,0:T(8,128)} %guess.1, s32[4,128,128]{2,1,0:T(8,128)} %mats.1, f32[8]{0:T(128)} %table.1, f32[4,128,128]{2,1,0:T(8,128)} %weight.1), custom_call_target="tpu_custom_call" | custom-call | tf_op jit(solution)/shard_map/pallas_call | solution.py:756
  105.3 0.0 copy-start
  105.3 0.9 reshape.10
  106.2 0.1 copy.7
  106.3 0.7 reshape.11
  107.0 0.0 copy-done
  107.0 0.7 copy.9
Async XLA Ops:
  105.3 1.7 %copy-start = (f32[1,4,128,128]{3,2,1,0:T(8,128)S(1)}, f32[1,4,128,128]{3,2,1,0:T(8,128)}, u32[]{:S(2)}) copy-start(f32[1,4,128,128]{3,2,1,0:T(8,128)} %get-tuple-element.8) | copy-start | bytes 786436

commit v5 on v4

--- a/solution.py
+++ b/solution.py
@@ -42,7 +42,7 @@
     ck, guess, mats, table, weight,
     out, sens_out,
     st, yh, ys, zh_, zs_, c0, c1, c2, c3, base_src, bb, wt, bwh, bws, bzh, bzs, g, cor, err, eyh, eys, ezh, ezs,
-    total, turned, sr, s2, sf, ids_, id_sem,
+    total, turned, sr, s2, sf, ids_, id_sem, own, own_sem,
     ck_send, ck_recv, gu_send, gu_recv, bs_send, bs_recv, wt_send, wt_recv,
     bx_send, bx_recv, ex_send, ex_recv, hop_send, hop_recv,
     ce_send, ce_recv, co_send, co_recv, r1_send, r1_recv, r2_send, r2_recv,
@@ -73,6 +73,12 @@
     barrier = pltpu.get_barrier_semaphore()
     fetch = pltpu.make_async_copy(mats, ids_, id_sem)
     fetch.start()
+    slabs = [
+        pltpu.make_async_copy(ref, own.at[n], own_sem.at[n])
+        for n, ref in enumerate((ck.at[0], guess.at[0], weight))
+    ]
+    for slab in slabs:
+        slab.start()
 
     def greet(px_, y_, z_):
         pl.semaphore_signal(barrier, inc=1, device_id=dev(px_, y_, z_), device_id_type=MESH)
@@ -181,6 +187,8 @@
         err[0] = jnp.zeros((PADP, PADR, LANES), F32)
         st[RELAX, 3, MID_P, MID_R] = jnp.zeros((PLANES, ROWS, LANES), F32)
 
+    for slab in slabs:
+        slab.wait()
     pl.semaphore_wait(barrier, count)
 
     def push(src, dst, ssem, rsem, px_, y_, z_):
@@ -219,12 +227,12 @@
 
     def send_ck(i, carry):
         z_ = turn(i)
-        push(cut(ck.at[0], z_), st.at[0, mine, pl.ds(H + 4 * half, 4), MID_R], ck_send.at[i], ck_recv.at[slot], to_px, y, z_)
+        push(cut(own.at[0], z_), st.at[0, mine, pl.ds(H + 4 * half, 4), MID_R], ck_send.at[i], ck_recv.at[slot], to_px, y, z_)
         return carry
 
     def send_guess(i, carry):
         z_ = turn(i)
-        push(cut(guess.at[0], z_), g.at[mine, pl.ds(4 * half, 4)], gu_send.at[i], gu_recv.at[slot], to_px, y, z_)
+        push(cut(own.at[1], z_), g.at[mine, pl.ds(4 * half, 4)], gu_send.at[i], gu_recv.at[slot], to_px, y, z_)
         return carry
 
     for i in range(2):
@@ -372,7 +380,7 @@
     batch_start(0)
     for i in range(2):
         z_ = 2 * mine + i
-        push(cut(weight, z_), wt.at[pl.ds(H + 4 * half, 4), MID_R], wt_send.at[i], wt_recv.at[half], to_px, y, z_)
+        push(cut(own.at[2], z_), wt.at[pl.ds(H + 4 * half, 4), MID_R], wt_send.at[i], wt_recv.at[half], to_px, y, z_)
     static_wait(0)
     batch_wait(0)
     lax.fori_loop(0, 4, send_guess, 0)
@@ -738,12 +746,12 @@
     for i in range(2):
         z_ = 2 * mine + i
         push_done(cut(base_src, z_), bs_send.at[i], to_px, y, z_)
-        push_done(cut(weight, z_), wt_send.at[i], to_px, y, z_)
+        push_done(cut(own.at[2], z_), wt_send.at[i], to_px, y, z_)
 
     def drain(i, carry):
         z_ = turn(i)
-        push_done(cut(ck.at[0], z_), ck_send.at[i], to_px, y, z_)
-        push_done(cut(guess.at[0], z_), gu_send.at[i], to_px, y, z_)
+        push_done(cut(own.at[0], z_), ck_send.at[i], to_px, y, z_)
+        push_done(cut(own.at[1], z_), gu_send.at[i], to_px, y, z_)
         return carry
 
     lax.fori_loop(0, 8, drain, 0)
@@ -801,6 +809,8 @@
             vmem(8, 8, LANES),
             pltpu.VMEM((4, 128, LANES), jnp.int32),
             dma,
+            vmem(3, 4, 128, LANES),
+            dma((3,)),
             dma((8,)), dma((8,)), dma((8,)), dma((8,)),
             dma((2,)), dma((2,)), dma((2,)), dma((2,)),
             dma((2, 8)), dma((2, 8)),

time: 109 us -> 109 us (level)
  no operation moved by 1% of the time
where the time goes in v5:
time: 109 us; the launch traced here: 107 us
  Pallas kernels  104 us (95%)
  local copies, waits for them, and re-layouts  2.41 us (2%)
    pallas_call x1, Pallas kernels, on_device(): pl.pallas_call(kernel, out_shape=(jax.ShapeDtypeStruct(guess.shape, F32),...  104 us

profile of v5, /device:TPU:17, one launch (start us, length us, event | category | flops | bytes accessed | tf_op | source)
XLA Modules:
  0.0 107.2 jit_solution(7670357587340251199)
XLA Ops:
  0.6 104.1 %shard_map.68 = (f32[1,4,128,128]{3,2,1,0:T(8,128)}, f32[8,8,128]{2,1,0:T(8,128)}) custom-call(f32[1,4,128,128]{3,2,1,0:T(8,128)} %ck.1, f32[1,4,128,128]{3,2,1,0:T(8,128)} %guess.1, s32[4,128,128]{2,1,0:T(8,128)} %mats.1, f32[8]{0:T(128)} %table.1, f32[4,128,128]{2,1,0:T(8,128)} %weight.1), custom_call_target="tpu_custom_call" | custom-call | tf_op jit(solution)/shard_map/pallas_call | solution.py:764
  104.8 0.0 copy-start
  104.8 0.9 reshape.10
  105.7 0.1 copy.7
  105.8 0.7 reshape.11
  106.5 0.0 copy-done
  106.5 0.7 copy.9
Async XLA Ops:
  104.8 1.7 %copy-start = (f32[1,4,128,128]{3,2,1,0:T(8,128)S(1)}, f32[1,4,128,128]{3,2,1,0:T(8,128)}, u32[]{:S(2)}) copy-start(f32[1,4,128,128]{3,2,1,0:T(8,128)} %get-tuple-element.8) | copy-start | bytes 786436
